TPU v7x, 512 devices: a whole 4x4x16 slice. The times are simulated.
512 devices in a mesh: seq: 8 (over y, core), mp: 64 (over z, x).
Axes of the slice: x: 4, y: 4, z: 16, core: 2. Of those that a mesh axis runs over, the one named last changes fastest.
Arguments:
- residual_in: bfloat16 [1024, 8192], P('seq', 'mp'), may hold values from -6 to 6
- ssm_input: bfloat16 [1024, 16384], P('seq', 'mp'), may hold values from -6 to 6
- gate_input: bfloat16 [1024, 16384], P('seq', 'mp'), may hold values from -6 to 6
- b_proj: bfloat16 [1024, 8, 256], P('seq'), may hold values from -6 to 6
- c_proj: bfloat16 [1024, 8, 256], P('seq'), may hold values from -6 to 6
- step_raw: float32 [1024, 256], P('seq', 'mp'), may hold values from -4.2 to 3.5
- decay_log: float32 [256], P('mp'), may hold values from -4.61 to 1.26
- skip_gain: float32 [256], P('mp'), may hold values from 0.5 to 2
- mixer_gain: float32 [16384], replicated, may hold values from 0.1 to 1.9
- out_weight: bfloat16 [16384, 8192], P('seq', 'mp'), may hold values from -0.046875 to 0.046875
- final_gain: float32 [8192], replicated, may hold values from 0.1 to 1.9
- head_weight: bfloat16 [8192, 65536], P('seq', 'mp'), may hold values from -24 to 24
- targets: int32 [1024], replicated, may hold values from 0 to 65535
- segment_ids: int32 [1024], replicated, may hold values from 0 to 1, as said below
- loss_mask: int32 [1024], replicated, may hold values from 0 to 1, as said below
Outputs:
- mixer_out: bfloat16 [1024, 8192], P('seq', 'mp')
- token_logp: float32 [1024], P('seq')
- response_logp: float32 [3], replicated
Inputs may be any that keep to these rules, and one draw needn't show every extreme that they name: `segment_ids`: 0 on the positions of the chosen response, then 1 on those of the rejected one; each response holds at least 256 positions. `loss_mask`: 1 at the first position of each response.
All inputs are finite; a program needn't handle non-finite values.
Results may differ from a plain program's by a relative error of at most 0.008.
Values may be sent and summed in bfloat16 or wider, within the bound.
No kernel may reach another device: no remote copies, remote signals or barrier semaphores. Data moves between devices by JAX's collectives and lax.ppermute only.
A program may use at most 64 MiB of HBM per device.

v0:
```python
import jax
import jax.numpy as jnp
from jax import lax
from jax.sharding import PartitionSpec as P

BLOCK = 64


EPS = 1e-05
HIGH = lax.Precision.HIGHEST


def prefix(array, axis, combine, identity):
    devices, here = (lax.axis_size(axis), lax.axis_index(axis))
    everything = jax.tree.map(lambda part: lax.all_gather(part, axis), array)
    start = jax.tree.map(
        lambda part, zero: jnp.broadcast_to(jnp.asarray(zero, part.dtype), part.shape),
        array,
        identity,
    )

    def step(k, before):
        reached = k < here
        new = combine(before, jax.tree.map(lambda part: part[k], everything))
        return jax.tree.map(lambda a, b: jnp.where(reached, a, b), new, before)

    return lax.fori_loop(0, devices, step, start)


def combined_all(part, axis, combine):
    gathered = jax.tree.map(lambda a: lax.all_gather(a, axis), part)

    def take(source):
        return jax.tree.map(lambda a: lax.dynamic_index_in_dim(a, source, 0, False), gathered)

    return lax.fori_loop(
        1, lax.axis_size(axis), lambda source, state: combine(state, take(source)), take(0)
    )


def state_combine(earlier, latter):
    return (earlier[0] * latter[0], latter[0][:, None, None] * earlier[1] + latter[1])


def softmax_combine(former, latter):
    top_value = jnp.maximum(former[0], latter[0])
    exp_mass = former[1] * jnp.exp(former[0] - top_value) + latter[1] * jnp.exp(
        latter[0] - top_value
    )
    return (top_value, exp_mass, former[2] + latter[2])


def block_pieces(inputs, step_size, log_decay, b_rows, c_rows, seg_rows, seg_before):
    stretch_span = inputs.shape[1]
    cumulative = jnp.cumsum(log_decay, axis=1)
    places = jnp.arange(stretch_span)
    causal = (places[:, None] >= places[None, :])[None] & (
        seg_rows[:, :, None] == seg_rows[:, None, :]
    )
    causal_heads = causal[..., None]
    gap_log = cumulative[:, :, None, :] - cumulative[:, None, :, :]
    weights = jnp.where(causal_heads, jnp.exp(jnp.where(causal_heads, gap_log, 0.0)), 0.0)
    scores = jnp.einsum("ctn,csn->cts", c_rows, b_rows, preferred_element_type=jnp.float32)
    scaled = step_size[..., None] * inputs
    inner_out = jnp.einsum("ctsh,cshp->cthp", scores[..., None] * weights, scaled, precision=HIGH)
    carry_in = jnp.where((seg_rows == seg_before[:, None])[..., None], jnp.exp(cumulative), 0.0)
    to_end = jnp.where(
        (seg_rows == seg_rows[:, -1:])[..., None], jnp.exp(cumulative[:, -1:, :] - cumulative), 0.0
    )
    added_state = jnp.einsum(
        "csh,cshp,csn->chpn", to_end, scaled, b_rows.astype(jnp.float32), precision=HIGH
    )
    carry_keep = jnp.where(
        (seg_rows[:, -1] == seg_before)[:, None], jnp.exp(cumulative[:, -1, :]), 0.0
    )
    return (inner_out, carry_in, carry_keep, added_state)


def response_terms(logp_rows, seg_rows, mask_rows):
    counted = mask_rows == 1
    totals = []
    counts = []
    for which in range(2):
        selected = counted & (seg_rows == which)
        totals.append(jnp.sum(jnp.where(selected, logp_rows, 0.0)))
        counts.append(jnp.sum(selected.astype(jnp.float32)))
    return (jnp.stack(totals), jnp.stack(counts))


def local(
    residual_in,
    ssm_input,
    gate_input,
    b_proj,
    c_proj,
    step_raw,
    decay_log,
    skip_gain,
    mixer_gain,
    out_weight,
    final_gain,
    head_weight,
    targets,
    segment_ids,
    loss_mask,
):
    tok_rows = ssm_input.shape[0]
    head_count = step_raw.shape[1]
    head_width = ssm_input.shape[1] // head_count
    state_size = b_proj.shape[2]
    group_count = b_proj.shape[1]
    total_rows = segment_ids.shape[0]
    vocab_count = head_weight.shape[1]
    seq_index = lax.axis_index("seq")
    mp_index = lax.axis_index("mp")
    row_start = seq_index * tok_rows
    block_count = tok_rows // BLOCK
    heads_group = head_count * lax.axis_size("mp") // group_count
    my_group = mp_index * head_count // heads_group
    b_rows = lax.dynamic_index_in_dim(b_proj, my_group, 1, keepdims=False)
    c_rows = lax.dynamic_index_in_dim(c_proj, my_group, 1, keepdims=False)
    inputs = ssm_input.astype(jnp.float32).reshape(block_count, BLOCK, head_count, head_width)
    step_size = jax.nn.softplus(step_raw)
    log_decay = -jnp.exp(decay_log)[None, :] * step_size
    boundary = total_rows - jnp.sum(segment_ids)
    places = row_start + jnp.arange(tok_rows, dtype=jnp.int32)
    seg_rows = (places >= boundary).astype(jnp.int32)
    before_place = jnp.maximum(row_start + jnp.arange(block_count, dtype=jnp.int32) * BLOCK - 1, 0)
    seg_before = (before_place >= boundary).astype(jnp.int32)
    inner_out, carry_in, carry_keep, added_state = block_pieces(
        inputs,
        step_size.reshape(block_count, BLOCK, head_count),
        log_decay.reshape(block_count, BLOCK, head_count),
        b_rows.reshape(block_count, BLOCK, state_size),
        c_rows.reshape(block_count, BLOCK, state_size),
        seg_rows.reshape(block_count, BLOCK),
        seg_before,
    )
    identity = (
        jnp.ones((head_count,), jnp.float32),
        jnp.zeros((head_count, head_width, state_size), jnp.float32),
    )

    def local_prefix(running, piece):
        return (state_combine(running, piece), running)

    device_total, block_prefix = lax.scan(local_prefix, identity, (carry_keep, added_state))
    entering = prefix(device_total, "seq", state_combine, identity)
    start_states = block_prefix[0][:, :, None, None] * entering[1][None] + block_prefix[1]
    outer_out = carry_in[..., None] * jnp.einsum(
        "ctn,chpn->cthp",
        c_rows.astype(jnp.float32).reshape(block_count, BLOCK, state_size),
        start_states,
        precision=HIGH,
    )
    ssd = (inner_out + outer_out).reshape(tok_rows, head_count, head_width) + skip_gain[
        None, :, None
    ] * inputs.reshape(tok_rows, head_count, head_width)
    gated = (
        ssd.reshape(tok_rows, head_count * head_width) * jax.nn.silu(gate_input.astype(jnp.float32))
    ).astype(jnp.bfloat16)
    gathered = lax.all_gather(gated, "mp", axis=1, tiled=True)
    grouped = gathered.astype(jnp.float32).reshape(tok_rows, group_count, -1)
    group_scale = lax.rsqrt(jnp.mean(grouped * grouped, axis=2) + EPS)
    mixer_normed = ((grouped * group_scale[:, :, None]).reshape(tok_rows, -1) * mixer_gain).astype(
        jnp.bfloat16
    )
    mixer_out = jnp.dot(
        mixer_normed,
        lax.all_gather(out_weight, "seq", axis=0, tiled=True),
        preferred_element_type=jnp.float32,
    ).astype(jnp.bfloat16)
    residual_sum = (residual_in.astype(jnp.float32) + mixer_out.astype(jnp.float32)).astype(
        jnp.bfloat16
    )
    whole_rows = lax.all_gather(residual_sum, "mp", axis=1, tiled=True)
    whole_float = whole_rows.astype(jnp.float32)
    row_scale = lax.rsqrt(jnp.mean(whole_float * whole_float, axis=1) + EPS)
    head_input = (whole_float * row_scale[:, None] * final_gain).astype(jnp.bfloat16)
    slices = lax.all_to_all(head_input, "seq", split_axis=1, concat_axis=0, tiled=True)
    logits = lax.psum_scatter(
        jnp.dot(slices, head_weight, preferred_element_type=jnp.float32),
        "seq",
        scatter_dimension=0,
        tiled=True,
    )
    vocab_ids = mp_index * vocab_count + jnp.arange(vocab_count, dtype=jnp.int32)
    own_targets = lax.dynamic_slice_in_dim(targets, row_start, tok_rows)
    target_hit = own_targets[:, None] == vocab_ids[None, :]
    top_local = jnp.max(logits, axis=1)
    mass_local = jnp.sum(jnp.exp(logits - top_local[:, None]), axis=1)
    picked_local = jnp.sum(jnp.where(target_hit, logits, 0.0), axis=1)
    top_value, exp_mass, picked = combined_all(
        (top_local, mass_local, picked_local), "mp", softmax_combine
    )
    token_logp = picked - (top_value + jnp.log(exp_mass))
    own_segments = lax.dynamic_slice_in_dim(segment_ids, row_start, tok_rows)
    own_mask = lax.dynamic_slice_in_dim(loss_mask, row_start, tok_rows)
    local_totals, local_counts = response_terms(token_logp, own_segments, own_mask)
    totals, counts = lax.psum((local_totals, local_counts), "seq")
    means = totals / counts
    response_logp = jnp.stack([means[0], means[1], means[0] - means[1]])
    return (mixer_out, token_logp, response_logp)


def solution(mesh):
    in_specs = (
        P("seq", "mp"),
        P("seq", "mp"),
        P("seq", "mp"),
        P("seq", None, None),
        P("seq", None, None),
        P("seq", "mp"),
        P("mp"),
        P("mp"),
        P(),
        P("seq", "mp"),
        P(),
        P("seq", "mp"),
        P(),
        P(),
        P(),
    )
    out_specs = (P("seq", "mp"), P("seq"), P())
    return jax.shard_map(local, mesh=mesh, in_specs=in_specs, out_specs=out_specs, check_vma=False)
```

profile of v0, /device:TPU:1, one launch (start us, length us, event | category | flops | bytes accessed | tf_op | source)
XLA Modules:
  0.0 728.9 jit_solution(10677477643664645686)
XLA Ops:
  7.2 1.5 reduce_sum.81
  9.9 1.5 constant_dynamic-slice_fusion.4
  14.9 4.2 while.54
  15.8 1.3 dynamic_update_slice.16
  17.9 1.3 dynamic_update_slice.16
  20.0 1.3 dynamic-slice
  22.1 18.8 %all-reduce = f32[32]{0:T(128)S(1)} all-reduce(f32[32]{0:T(128)S(1)} %dynamic-update-slice), channel_id=2, replica_groups=mesh['seq'=8,'mp'=64] {'seq'}, use_global_device_ids=true, to_apply=%add | all-reduce | flops 32 | bytes 256
  42.8 15.8 %all-gather.19.cloned.1.call-done = f32[32,64,256]{2,1,0:T(8,128)} async-done(((f32[4,64,256]{2,1,0:T(8,128)}), f32[32,64,256]{2,1,0:T(8,128)}) %all-gather.19.cloned.1.call-update) | async-done | bytes 2097168 | tf_op jit(solution)/shard_map/all_gather | solution.py:15
  58.6 8.7 %while.55 = (s32[]{:T(128)}, f32[4,64,256]{2,1,0:T(8,128)S(1)}, s32[]{:T(128)}, f32[8,4]{1,0:T(8,128)S(1)}, f32[8,4,64,256]{3,2,1,0:T(8,128)}) while((s32[]{:T(128)}, f32[4,64,256]{2,1,0:T(8,128)S(1)}, s32[]{:T(128)}, f32[8,4]{1,0:T(8,128)S(1)}, f32[8,4,64,256]{3,2,1,0:T(8,128)}) %tuple.134), condition=%wide.region_5.6_spmd.clone.clone, body=%wide.region_4.5_spmd.clone.sunk.clone | while | flops 262148 | bytes 786569 | solution.py:27
  67.4 1.5 fusion.19
  69.2 1.5 fusion.47
  71.7 135.6 %all-gather.13.cloned.1.call-done = bf16[128,16384]{1,0:T(8,128)(2,1)} async-done(((bf16[128,256]{1,0:T(8,128)(2,1)}), bf16[128,16384]{1,0:T(8,128)(2,1)}) %all-gather.13.cloned.1.call-update) | async-done | bytes 4194320 | tf_op jit(solution)/shard_map/all_gather | solution.py:162
  207.4 3.1 convert_multiply_fusion.1
  210.5 9.7 %copy.109 = f32[16,8,8,2048]{3,2,1,0:T(8,128)} copy(f32[16,8,8,2048]{3,1,2,0:T(8,128)S(1)} %bitcast.102) | data formatting | bytes 16777216
  220.2 3.8 reduce_sum.82
  224.8 9.9 %copy.110 = f32[16,8,8,2048]{3,1,2,0:T(8,128)} copy(f32[16,8,8,2048]{3,2,1,0:T(8,128)S(1)} %bitcast.101) | data formatting | bytes 16777216
  234.8 18.3 %all-gather.15.cloned.1.call-done = bf16[16384,128]{1,0:T(8,128)(2,1)} async-done(((bf16[2048,128]{1,0:T(8,128)(2,1)}), bf16[16384,128]{1,0:T(8,128)(2,1)}) %all-gather.15.cloned.1.call-update) | async-done | bytes 4194320 | tf_op jit(solution)/shard_map/all_gather | solution.py:170
  253.0 7.9 %add_convert_fusion = (bf16[128,128]{1,0:T(8,128)(2,1)}, bf16[128,128]{1,0:T(8,128)(2,1)}) fusion(bf16[128,128]{1,0:T(8,128)(2,1)S(1)} %copy-done.4, bf16[16384,128]{1,0:T(8,128)(2,1)} %all-gather.15.cloned.1.call-done, f32[128,16384]{1,0:T(8,128)} %bitcast.99, bf16[128,16384]{1,0:T(8,128)(2,1)} %all-gather.13.cloned.1.call-done, f32[16384]{0:T(1024)S(1)} %copy-done.3), kind=kOutput, calls=%fused_computation.66 | convolution fusion | flops 545341440 | bytes 16941056 | tf_op jit(solution)/shard_map/dot_general | solution.py:168
  261.0 125.9 %all-gather.17.cloned.1.call-done = bf16[128,8192]{1,0:T(8,128)(2,1)} async-done(((bf16[128,128]{1,0:T(8,128)(2,1)}), bf16[128,8192]{1,0:T(8,128)(2,1)}) %all-gather.17.cloned.1.call-update) | async-done | bytes 2097168 | tf_op jit(solution)/shard_map/all_gather | solution.py:176
  386.8 2.1 fusion.13
  388.9 2.2 fusion.15
  391.3 40.3 %all_to_all.19 = bf16[128,8,1024]{2,0,1:T(8,128)(2,1)S(1)} all-to-all(bf16[128,8,1024]{2,0,1:T(8,128)(2,1)S(1)} %bitcast.104), channel_id=1, replica_groups=mesh['seq'=8,'mp'=64] {'seq'}, dimensions={1} | all-to-all | bytes 4194304 | tf_op jit(solution)/shard_map/all_to_all | solution.py:180
  431.6 4.3 fusion.54
  437.5 36.8 %reduce-scatter.2.cloned.1.call-done = f32[128,1024]{1,0:T(8,128)} async-done(((f32[1024,1024]{1,0:T(8,128)}), f32[128,1024]{1,0:T(8,128)}) %reduce-scatter.2.cloned.1.call-update) | async-done | bytes 524304 | tf_op jit(solution)/shard_map/reduce_scatter | solution.py:181
  475.5 1.3 select_reduce_fusion
  476.8 59.6 %all-gather.7 = f32[64,1,128]{2,1,0:T(1,128)S(1)} all-gather(f32[1,1,128]{2,1,0:T(1,128)S(1)} %bitcast.119), channel_id=6, replica_groups=mesh['seq'=8,'mp'=64] {'mp'}, dimensions={0}, use_global_device_ids=true | all-gather | bytes 33280 | tf_op jit(solution)/shard_map/all_gather | solution.py:31
  536.4 54.7 %all-gather.6 = f32[64,1,128]{2,1,0:T(1,128)S(1)} all-gather(f32[1,1,128]{2,1,0:T(1,128)S(1)} %bitcast.118), channel_id=5, replica_groups=mesh['seq'=8,'mp'=64] {'mp'}, dimensions={0}, use_global_device_ids=true | all-gather | bytes 33280 | tf_op jit(solution)/shard_map/all_gather | solution.py:31
  591.1 55.9 %all-gather.5 = f32[64,1,128]{2,1,0:T(1,128)S(1)} all-gather(f32[1,1,128]{2,1,0:T(1,128)S(1)} %bitcast.117), channel_id=4, replica_groups=mesh['seq'=8,'mp'=64] {'mp'}, dimensions={0}, use_global_device_ids=true | all-gather | bytes 33280 | tf_op jit(solution)/shard_map/all_gather | solution.py:31
  647.0 3.0 while.53
  651.2 1.4 pad_maximum_fusion.1
  652.6 1.3 pad_maximum_fusion
  653.9 66.0 %all-reduce.1 = (f32[2]{0:T(128)S(1)}, f32[2]{0:T(128)S(1)}) all-reduce(f32[2]{0:T(128)S(1)} %pad_maximum_fusion, f32[2]{0:T(128)S(1)} %pad_maximum_fusion.1), channel_id=1, replica_groups=mesh['seq'=8,'mp'=64] {'seq'}, use_global_device_ids=true, to_apply=%region_16.17 | all-reduce | flops 4 | bytes 32 | tf_op jit(solution)/shard_map/psum | solution.py:200
  (164 shorter events, 26.5 us)
Async XLA Ops:
  7.2 424.5 %copy-start = (bf16[1024,1024]{1,0:T(8,128)(2,1)S(1)}, bf16[1024,1024]{1,0:T(8,128)(2,1)}, u32[]{:S(2)}) copy-start(bf16[1024,1024]{1,0:T(8,128)(2,1)} %param.32) | copy-start | bytes 6291460
  7.2 51.5 %all-gather.19.cloned.1.call-start = ((), (), s32[]{:S(2)}) async-start(), calls=%async_computation.6 | async-start | bytes 2359296 | tf_op jit(solution)/shard_map/all_gather | solution.py:15
  19.2 0.7 copy-start.1
  19.2 50.0 %copy-start.2 = (bf16[128,256]{1,0:T(8,128)(2,1)S(1)}, bf16[128,256]{1,0:T(8,128)(2,1)}, u32[]{:S(2)}) copy-start(bf16[128,256]{1,0:T(8,128)(2,1)} %param.22) | copy-start | bytes 196612
  19.9 187.5 %all-gather.13.cloned.1.call-start = ((), (), s32[]{:S(2)}) async-start(), calls=%async_computation.2 | async-start | bytes 4259840 | tf_op jit(solution)/shard_map/all_gather | solution.py:162
  22.1 45.2 %copy-start.6 = (f32[2,4]{1,0:T(2,128)S(1)}, f32[2,4]{1,0:T(2,128)}, u32[]{:S(2)}) copy-start(f32[2,4]{1,0:T(2,128)} %get-tuple-element.315) | copy-start | bytes 100
  70.8 182.3 %all-gather.15.cloned.1.call-start = ((), (), s32[]{:S(2)}) async-start(), calls=%async_computation.3 | async-start | bytes 4718592 | tf_op jit(solution)/shard_map/all_gather | solution.py:170
  71.5 315.3 %all-gather.17.cloned.1.call-start = ((), (), s32[]{:S(2)}) async-start(), calls=%async_computation.4 | async-start | bytes 2129920 | tf_op jit(solution)/shard_map/all_gather | solution.py:176
  224.8 28.2 %copy-start.3 = (f32[16384]{0:T(1024)S(1)}, f32[16384]{0:T(1024)}, u32[]{:S(2)}) copy-start(f32[16384]{0:T(1024)} %param.29) | copy-start | bytes 196612
  224.8 28.2 %copy-start.4 = (bf16[128,128]{1,0:T(8,128)(2,1)S(1)}, bf16[128,128]{1,0:T(8,128)(2,1)}, u32[]{:S(2)}) copy-start(bf16[128,128]{1,0:T(8,128)(2,1)} %param.21) | copy-start | bytes 98308
  253.0 135.9 %copy-start.5 = (f32[8192]{0:T(1024)S(1)}, f32[8192]{0:T(1024)}, u32[]{:S(2)}) copy-start(f32[8192]{0:T(1024)} %param.31) | copy-start | bytes 98308
  260.9 213.4 %reduce-scatter.2.cloned.1.call-start = ((), (), s32[]{:S(2)}) async-start(), calls=%async_computation.5 | async-start | bytes 4718592 | tf_op jit(solution)/shard_map/reduce_scatter | solution.py:181
Sparse Core Ops, SparseCore 0:
  20.0 38.5 all-gather.18
  70.9 136.4 all-gather.12
  209.5 43.4 all-gather.14
  261.0 125.7 all-gather.16
  436.1 38.2 reduce-scatter.1
where the time goes:
time: 730 us; the launch traced here: 729 us
  waiting for transfers between devices  333 us (46%)
  blocking collectives  295 us (40%)
  other arithmetic  35.9 us (5%)
  local copies, waits for them, and re-layouts  31.4 us (4%)
  between operations  16.6 us (2%)
  matrix products  14.8 us (2%)
    all_gather x3, blocking collectives, combined_all(): gathered = jax.tree.map(lambda a: lax.all_gather(a, axis), part)  170 us
    all_gather x1, waiting for transfers between devices, local(): gathered = lax.all_gather(gated, 'mp', axis=1, tiled=True)  136 us
    all_gather x1, waiting for transfers between devices, local(): whole_rows = lax.all_gather(residual_sum, 'mp', axis=1, tiled=True)  126 us
    psum x1, blocking collectives, local(): totals, counts = lax.psum((local_totals, local_counts), 'seq')  66 us
    all_to_all x1, blocking collectives, local(): lax.all_to_all(head_input, 'seq', split_axis=1, concat_axis=0, tiled=True)  40.3 us
    reduce_scatter x1, waiting for transfers between devices, local(): lax.psum_scatter(jnp.dot(slices, head_weight, preferred_element_type=jnp....  36.8 us
    unnamed x21, local copies, waits for them, and re-layouts  21.9 us
    unnamed x1, blocking collectives  18.8 us
  transfers between devices with their start and end apart: 5, of which 5 were waited for; matrix products, arithmetic and copies ran while one was open for 4% of the time, Pallas kernels for 0%

commit v1 on v0

v1 whole, which is shorter than its diff:
```python
import jax
import jax.numpy as jnp
from jax import lax
from jax.experimental import pallas as pl
from jax.experimental.pallas import tpu as pltpu
from jax.sharding import Mesh, PartitionSpec as P

EPS = 1e-05
HIGH = lax.Precision.HIGHEST
F32 = jnp.float32
BF16 = jnp.bfloat16

NY, NC, NG, NL, NX = (4, 2, 8, 2, 4)
NZ = NG * NL
AXES = ("y", "core", "zg", "zl", "x")
SEQ = ("y", "core")
MP = ("zg", "zl", "x")
ROWS = 128
HEADS = 4
WIDTH = 64
CHANNELS = HEADS * WIDTH
STATE = 256
GROUPS = 8
MSG = STATE + 16


def dot(a, b, precision=None):
    return jnp.dot(a, b, preferred_element_type=F32, precision=precision)


def vmem():
    return pl.BlockSpec(memory_space=pltpu.VMEM)


def smem():
    return pl.BlockSpec(memory_space=pltpu.SMEM)


def call(body, out_shape, specs):
    many = isinstance(out_shape, (tuple, list))
    return pl.pallas_call(
        body,
        out_shape=out_shape,
        in_specs=specs,
        out_specs=[vmem() for _ in out_shape] if many else vmem(),
        compiler_params=pltpu.CompilerParams(vmem_limit_bytes=32 * 1024 * 1024),
    )


def head_columns(columns):
    lane = lax.broadcasted_iota(jnp.int32, (ROWS, CHANNELS), 1) // WIDTH
    wide = jnp.broadcast_to(columns[0], (ROWS, CHANNELS))
    for h in range(1, HEADS):
        wide = jnp.where(lane == h, columns[h], wide)
    return wide


def scan_kernel(place, seg, step_raw, decay_log, skip, x_ref, b_ref, c_ref, inner, carry, msg):
    row_start = place[0] * ROWS
    boundary = seg.shape[0] * seg.shape[1] - jnp.sum(seg[...])
    raw = step_raw[...]
    step = jnp.maximum(raw, 0.0) + jnp.log1p(jnp.exp(-jnp.abs(raw)))
    log_decay = -jnp.exp(decay_log[...]) * step
    share = ROWS // HEADS
    lane = lax.broadcasted_iota(jnp.int32, (ROWS, ROWS), 1)
    row = lax.broadcasted_iota(jnp.int32, (ROWS, ROWS), 0)
    spread = jnp.broadcast_to(log_decay[:, 0:1], (ROWS, ROWS))
    for h in range(1, HEADS):
        spread = jnp.where(lane // share == h, log_decay[:, h : h + 1], spread)
    below = (row >= lane).astype(F32)
    total = dot(below, spread, HIGH)
    total_t = total.T
    columns = [total[:, share * h : share * h + 1] for h in range(HEADS)]
    wide = head_columns(columns)
    places = row_start + lax.broadcasted_iota(jnp.int32, (ROWS, 1), 0)
    seg_rows = (places >= boundary).astype(jnp.int32)
    seg_lanes = (row_start + lane >= boundary).astype(jnp.int32)
    seg_before = (jnp.maximum(row_start - 1, 0) >= boundary).astype(jnp.int32)
    seg_last = (row_start + ROWS - 1 >= boundary).astype(jnp.int32)
    allowed = (row >= lane) & (seg_rows == seg_lanes)
    inputs = x_ref[...].astype(F32)
    scaled = head_columns([step[:, h : h + 1] for h in range(HEADS)]) * inputs
    scores = lax.dot_general(
        c_ref[...], b_ref[...], (((1,), (1,)), ((), ())), preferred_element_type=F32
    )
    for h in range(HEADS):
        gap = columns[h] - total_t[share * h : share * h + 1, :]
        weight = jnp.where(allowed, jnp.exp(jnp.where(allowed, gap, 0.0)), 0.0)
        part = slice(h * WIDTH, (h + 1) * WIDTH)
        inner[:, part] = dot(scores * weight, scaled[:, part], HIGH)
    inner[...] += skip[...] * inputs
    carry[...] = jnp.where(seg_rows == seg_before, jnp.exp(wide), 0.0)
    last = wide[ROWS - 1 : ROWS, :]
    to_end = jnp.where(seg_rows == seg_last, jnp.exp(last - wide), 0.0)
    msg[0:STATE, :] = lax.dot_general(
        b_ref[...].astype(F32),
        scaled * to_end,
        (((0,), (0,)), ((), ())),
        preferred_element_type=F32,
        precision=HIGH,
    )
    keep = jnp.where(seg_last == seg_before, jnp.exp(last), 0.0)
    msg[STATE : STATE + 8, :] = jnp.broadcast_to(keep, (8, CHANNELS))


def chip_kernel(pair, out):
    keep = [pair[k, STATE : STATE + 1, :] for k in range(NC)]
    out[0:STATE, :] = (keep[1] * pair[0, 0:STATE, :] + pair[1, 0:STATE, :]).astype(BF16)
    both = keep[0] * keep[1]
    coarse = both.astype(BF16).astype(F32)
    line = lax.broadcasted_iota(jnp.int32, (MSG - STATE, CHANNELS), 0)
    out[STATE:MSG, :] = jnp.where(line == 0, coarse, jnp.where(line == 1, both - coarse, 0.0)).astype(
        BF16
    )


def gate_kernel(place, chips, pair, c_ref, inner, carry, gate, out, squares):
    y, core = (place[1], place[2])
    state = jnp.zeros((STATE, CHANNELS), F32)
    for k in range(NY - 1):
        tail = chips[k, STATE:MSG, :].astype(F32)
        keep = tail[0:1, :] + tail[1:2, :]
        state = jnp.where(k < y, keep * state + chips[k, 0:STATE, :].astype(F32), state)
    state = jnp.where(
        core == 1, pair[0, STATE : STATE + 1, :] * state + pair[0, 0:STATE, :], state
    )
    ssd = inner[...] + carry[...] * dot(c_ref[...].astype(F32), state, HIGH)
    v = gate[...].astype(F32)
    gated = (ssd * (v / (1.0 + jnp.exp(-v)))).astype(BF16)
    out[...] = gated
    rounded = gated.astype(F32)
    column = jnp.sum(rounded * rounded, axis=1, keepdims=True)
    squares[...] = jnp.broadcast_to(column, (ROWS, ROWS)).T[0:8, :]


def norm_kernel(place, gated, squares, gain, out):
    line = jnp.sum(squares[...], axis=0, keepdims=True)
    scale = lax.rsqrt(jnp.broadcast_to(line, (ROWS, ROWS)).T / 2048.0 + EPS)
    wide = jnp.concatenate([scale] * (CHANNELS // ROWS), axis=1)
    out[...] = (gated[...].astype(F32) * wide * gain[pl.ds(place[5], 1), :]).astype(BF16)


def project_kernel(other, place, rows, weight, *rest):
    before, out = rest if other else (None,) + rest
    side = lax.rem(place[6] + other, NL)
    total = before[...] if other else jnp.zeros((ROWS, NX * ROWS), F32)
    for g in range(NG):
        total = total + dot(
            rows[g], jnp.concatenate([weight[g, k, side] for k in range(NX)], axis=1)
        )
    if other:
        for k in range(NX):
            out[k] = total[:, k * ROWS : (k + 1) * ROWS]
    else:
        out[...] = total


def project(place, rows, weight, before=None):
    other = 0 if before is None else 1
    return pl.pallas_call(
        lambda *refs: project_kernel(other, *refs),
        out_shape=jax.ShapeDtypeStruct((NX, ROWS, ROWS) if other else (ROWS, NX * ROWS), F32),
        in_specs=[smem()] + [vmem()] * (2 + other),
        out_specs=vmem(),
        cost_estimate=pl.CostEstimate(
            flops=2 * ROWS * NG * CHANNELS * NX * ROWS, bytes_accessed=1 << 22, transcendentals=0
        ),
        compiler_params=pltpu.CompilerParams(vmem_limit_bytes=32 * 1024 * 1024),
    )(place, rows, weight, *([before] if other else []))


def residual_kernel(parts, residual, mixer_out, summed):
    mixed = ((parts[0] + parts[1]) + (parts[2] + parts[3])).astype(BF16)
    mixer_out[...] = mixed
    summed[...] = (residual[...].astype(F32) + mixed.astype(F32)).astype(BF16)


def head_kernel(place, p0, p1, p2, p3, gain, wanted, weight, out, total, squares):
    s = pl.program_id(0)

    @pl.when(s == 0)
    def _():
        total[...] = jnp.zeros_like(total)
        squares[...] = jnp.zeros_like(squares)

    square = jnp.zeros((ROWS, ROWS), F32)
    result = total[...]
    for k, part in enumerate((p0, p1, p2, p3)):
        source = lax.rem(place[4] + NX - k, NX)
        blocks = []
        for half in range(NL):
            v = part[half].astype(F32)
            square = square + v * v
            blocks.append((v * gain[half, source]).astype(BF16))
        pieces = [weight[0, half, source] for half in range(NL)]
        result = result + dot(
            jnp.concatenate(blocks, axis=1), jnp.concatenate(pieces, axis=0)
        )
    total[...] = result
    squares[...] += square

    @pl.when(s == pl.num_programs(0) - 1)
    def _():
        mean = jnp.sum(squares[...], axis=1, keepdims=True) / 8192.0
        logits = total[...] * lax.rsqrt(mean + EPS)
        top = jnp.max(logits, axis=1, keepdims=True)
        mass = jnp.sum(jnp.exp(logits - top), axis=1, keepdims=True)
        first = place[5] * logits.shape[1]
        vocab = first + lax.broadcasted_iota(jnp.int32, logits.shape, 1)
        picked = jnp.sum(jnp.where(vocab == wanted[...], logits, 0.0), axis=1, keepdims=True)
        lane = lax.broadcasted_iota(jnp.int32, (ROWS, ROWS), 1)
        out[...] = jnp.where(lane % 2 == 0, top + jnp.log(mass), picked).T


def head(place, parts, gain, wanted, weight):
    columns = weight.shape[-1]
    return pl.pallas_call(
        head_kernel,
        grid=(NG,),
        out_shape=jax.ShapeDtypeStruct((ROWS, ROWS), F32),
        in_specs=[smem()]
        + [pl.BlockSpec((NL, ROWS, ROWS), lambda s: (s, 0, 0))] * NX
        + [
            pl.BlockSpec((NL, NX, 1, ROWS), lambda s: (s, 0, 0, 0)),
            pl.BlockSpec((ROWS, 1), lambda s: (0, 0)),
            pl.BlockSpec((1, NL, NX, ROWS, columns), lambda s: (s, 0, 0, 0, 0)),
        ],
        out_specs=pl.BlockSpec((ROWS, ROWS), lambda s: (0, 0)),
        scratch_shapes=[pltpu.VMEM((ROWS, columns), F32), pltpu.VMEM((ROWS, ROWS), F32)],
        cost_estimate=pl.CostEstimate(
            flops=2 * ROWS * NX * NZ * ROWS * columns, bytes_accessed=18 << 20, transcendentals=0
        ),
        compiler_params=pltpu.CompilerParams(vmem_limit_bytes=52 * 1024 * 1024),
    )(place, *parts, gain, wanted, weight)


def token_kernel(place, stats, seg, mask, logp, sums):
    even = lax.broadcasted_iota(jnp.int32, (ROWS, ROWS), 0) % 2 == 0
    table = stats[...]
    least = jnp.where(even, table, -jnp.inf)
    top = jnp.max(least, axis=0, keepdims=True)
    mass = jnp.sum(jnp.where(even, jnp.exp(least - top), 0.0), axis=0, keepdims=True)
    picked = jnp.sum(jnp.where(even, 0.0, table), axis=0, keepdims=True)
    value = picked - (top + jnp.log(mass))
    logp[...] = value
    mine = pl.ds(place[0], 1)
    counted = mask[mine, :] == 1
    lane = lax.broadcasted_iota(jnp.int32, (8, ROWS), 1)
    both = jnp.zeros((8, ROWS), F32)
    for k in range(2):
        chosen = jnp.where(counted & (seg[mine, :] == k), value, 0.0)
        both = jnp.where(lane == k, jnp.sum(chosen, axis=1, keepdims=True), both)
    sums[...] = both


def mean_kernel(sums, seg, mask, out):
    every = jnp.sum(sums[...], axis=0, keepdims=True)
    means = []
    for k in range(2):
        count = jnp.sum(jnp.where((mask[...] == 1) & (seg[...] == k), 1.0, 0.0))
        means.append(every[:, k : k + 1] / count)
    lane = lax.broadcasted_iota(jnp.int32, (1, ROWS), 1)
    out[...] = jnp.where(
        lane == 0, means[0], jnp.where(lane == 1, means[1], means[0] - means[1])
    )


def shifted(part, axis, k):
    n = lax.axis_size(axis)
    return lax.ppermute(part, axis, [(i, (i + k) % n) for i in range(n)])


def local(
    residual_in,
    ssm_input,
    gate_input,
    b_proj,
    c_proj,
    step_raw,
    decay_log,
    skip_gain,
    mixer_gain,
    out_weight,
    final_gain,
    head_weight,
    targets,
    segment_ids,
    loss_mask,
):
    y, core, zl, x = [lax.axis_index(axis) for axis in ("y", "core", "zl", "x")]
    group = lax.axis_index("zg")
    z = group * NL + zl
    seq = y * NC + core
    place = jnp.stack([seq, y, core, z, x, z * NX + x, zl]).astype(jnp.int32)
    seg = segment_ids.reshape(-1, ROWS)
    mask = loss_mask.reshape(-1, ROWS)
    b_rows = lax.dynamic_index_in_dim(b_proj, group, 1, keepdims=False)
    c_rows = lax.dynamic_index_in_dim(c_proj, group, 1, keepdims=False)

    inner, carry, msg = call(
        scan_kernel,
        (
            jax.ShapeDtypeStruct((ROWS, CHANNELS), F32),
            jax.ShapeDtypeStruct((ROWS, CHANNELS), F32),
            jax.ShapeDtypeStruct((STATE + 8, CHANNELS), F32),
        ),
        [smem()] + [vmem()] * 7,
    )(
        place,
        seg,
        step_raw,
        decay_log.reshape(1, HEADS),
        jnp.repeat(skip_gain, WIDTH).reshape(1, CHANNELS),
        ssm_input,
        b_rows,
        c_rows,
    )
    turned = lax.all_to_all(out_weight.reshape(NL, NX, CHANNELS, ROWS), "x", 1, 0)
    out_rows = lax.all_gather(turned, SEQ)
    head_rows = lax.all_gather(head_weight, SEQ)

    pair = lax.all_gather(msg, "core")
    chip = call(chip_kernel, jax.ShapeDtypeStruct((MSG, CHANNELS), BF16), [vmem()])(pair)
    chips = lax.all_gather(chip, "y")
    gated, squares = call(
        gate_kernel,
        (
            jax.ShapeDtypeStruct((ROWS, CHANNELS), BF16),
            jax.ShapeDtypeStruct((8, ROWS), F32),
        ),
        [smem()] + [vmem()] * 6,
    )(place, chips, pair, c_rows, inner, carry, gate_input)
    squares = lax.all_to_all(squares, ("zl", "x"), 0, 0, tiled=True)
    normed = call(
        norm_kernel, jax.ShapeDtypeStruct((ROWS, CHANNELS), BF16), [smem()] + [vmem()] * 3
    )(place, gated, squares, mixer_gain.reshape(-1, CHANNELS))
    same = lax.all_gather(normed, "zg")
    other = shifted(same, "zl", 1)
    total = project(place, same, out_rows)
    parts = lax.all_to_all(project(place, other, out_rows, total), "x", 0, 0)
    half = jax.ShapeDtypeStruct((ROWS, ROWS), BF16)
    mixer_out, summed = call(residual_kernel, (half, half), [vmem()] * 2)(parts, residual_in)

    column = lax.all_gather(summed, ("zg", "zl"))
    features = [column] + [shifted(column, "x", k) for k in range(1, NX)]
    wanted = lax.dynamic_slice_in_dim(targets, seq * ROWS, ROWS).reshape(ROWS, 1)
    gains = final_gain.reshape(NZ, NX, 1, ROWS)
    matrix = head_rows.reshape(NG, NL, NX, ROWS, -1)
    stats = head(place, features, gains, wanted, matrix)
    stats = lax.all_to_all(stats, MP, 0, 0, tiled=True)
    logp, sums = call(
        token_kernel,
        (jax.ShapeDtypeStruct((1, ROWS), F32), jax.ShapeDtypeStruct((8, ROWS), F32)),
        [smem()] + [vmem()] * 3,
    )(place, stats, seg, mask)
    sums = lax.all_to_all(sums, SEQ, 0, 0, tiled=True)
    means = call(mean_kernel, jax.ShapeDtypeStruct((1, ROWS), F32), [vmem()] * 3)(sums, seg, mask)
    return (mixer_out, logp.reshape(ROWS), means[0, :3])


def solution(mesh):
    fine = Mesh(mesh.devices.reshape(NY, NC, NG, NL, NX), AXES)
    mp = MP
    in_specs = (
        P(SEQ, mp),
        P(SEQ, mp),
        P(SEQ, mp),
        P(SEQ, None, None),
        P(SEQ, None, None),
        P(SEQ, mp),
        P(mp),
        P(mp),
        P(),
        P(SEQ, mp),
        P(),
        P(SEQ, mp),
        P(),
        P(),
        P(),
    )
    out_specs = (P(SEQ, mp), P(SEQ), P())
    return jax.shard_map(local, mesh=fine, in_specs=in_specs, out_specs=out_specs, check_vma=False)
```

time: 730 us -> 220 us (0.30)
  waiting for transfers between devices: 333 us -> 31.3 us
  blocking collectives: 295 us -> 135 us
  other arithmetic: 35.9 us -> 0 us
  local copies, waits for them, and re-layouts: 31.4 us -> 6.49 us
  Pallas kernels: 0 us -> 18.1 us
  matrix products: 14.8 us -> 0 us
  starting transfers between devices: 0.38 us -> 14.1 us
    all_gather x4 -> x2, waiting for transfers between devices: 296 us -> 9.77 us  [the longest x1 9.75 us: local(): head_rows = lax.all_gather(head_weight, SEQ)]
    all_gather x3 -> x4, blocking collectives: 170 us -> 75.7 us  [the longest x1 31.3 us: local(): same = lax.all_gather(normed, 'zg')]
    psum x1 -> x0, blocking collectives: 66 us -> none  [local(): totals, counts = lax.psum((local_totals, local_counts), 'seq')]
    reduce_scatter x1 -> x0, waiting for transfers between devices: 36.8 us -> none  [local(): lax.psum_scatter(jnp.dot(slices, head_weight, preferred_element_type=jnp....]
    all_to_all x1 -> x4, blocking collectives: 40.3 us -> 59.4 us  [the longest x1 29.2 us: local(): stats = lax.all_to_all(stats, MP, 0, 0, tiled=True)]
    unnamed x21 -> x31, local copies, waits for them, and re-layouts: 21.9 us -> 2.93 us
    unnamed x1 -> x0, blocking collectives: 18.8 us -> none
    pallas_call x0 -> x10, Pallas kernels: none -> 18.1 us  [the longest x1 10 us: head(): pl.pallas_call(head_kernel, grid=(NG,), out_shape=jax.ShapeDtypeStruct((R...]
  transfers between devices with their start and end apart: 5 -> 7, of which waited for: 5 -> 5; matrix products, arithmetic and copies ran while one was open for 4% -> 1% of each run, Pallas kernels for 0% -> 3%
where the time goes in v1:
time: 220 us; the launch traced here: 219 us
  blocking collectives  135 us (61%)
  waiting for transfers between devices  31.3 us (14%)
  Pallas kernels  18.1 us (8%)
  between operations  14.3 us (6%)
  starting transfers between devices  14.1 us (6%)
  local copies, waits for them, and re-layouts  6.49 us (3%)
    all_gather x1, blocking collectives, local(): same = lax.all_gather(normed, 'zg')  31.3 us
    all_to_all x1, blocking collectives, local(): stats = lax.all_to_all(stats, MP, 0, 0, tiled=True)  29.2 us
    all_gather x1, blocking collectives, local(): column = lax.all_gather(summed, ('zg', 'zl'))  26.3 us
    ppermute x4, waiting for transfers between devices, shifted(): return lax.ppermute(part, axis, [(i, (i + k) % n) for i in range(n)])  16 us
    all_to_all x1, blocking collectives, local(): lax.all_to_all(out_weight.reshape(NL, NX, CHANNELS, ROWS), 'x', 1, 0)  11.8 us
    ppermute x4, starting transfers between devices, shifted(): return lax.ppermute(part, axis, [(i, (i + k) % n) for i in range(n)])  10.7 us
    all_to_all x1, blocking collectives, local(): sums = lax.all_to_all(sums, SEQ, 0, 0, tiled=True)  10.4 us
    pallas_call x1, Pallas kernels, head(): pl.pallas_call(head_kernel, grid=(NG,), out_shape=jax.ShapeDtypeStruct((R...  10 us
  transfers between devices with their start and end apart: 7, of which 5 were waited for; matrix products, arithmetic and copies ran while one was open for 1% of the time, Pallas kernels for 3%

profile of v1, /device:TPU:1, one launch (start us, length us, event | category | flops | bytes accessed | tf_op | source)
XLA Modules:
  0.0 219.3 jit_solution(3331665739141827057)
XLA Ops:
  7.3 1.1 copy.37
  8.4 11.8 %all_to_all.53 = bf16[1,2,4,256,128]{4,3,1,0,2:T(8,128)(2,1)} all-to-all(bf16[1,2,4,256,128]{4,3,1,0,2:T(8,128)(2,1)S(1)} %copy.37), channel_id=1, replica_groups=mesh['y'=4,'core'=2,'zg'=8,'zl'=2,'x'=4] {'x'}, dimensions={2} | all-to-all | bytes 1048576 | tf_op jit(solution)/shard_map/all_to_all | solution.py:318
  20.3 0.7 all-gather.11.cloned.1.call-update
  21.3 1.5 constant_dynamic-slice_fusion
  22.9 1.7 shard_map.166
  24.6 8.2 %all-gather = f32[528,256]{1,0:T(8,128)S(1)} all-gather(f32[264,256]{1,0:T(8,128)S(1)} %get-tuple-element.12), channel_id=2, replica_groups=mesh['y'=4,'core'=2,'zg'=8,'zl'=2,'x'=4] {'core'}, dimensions={0}, use_global_device_ids=true | all-gather | bytes 811008 | tf_op jit(solution)/shard_map/all_gather | solution.py:322
  32.9 10.0 %all-gather.1 = bf16[1088,256]{1,0:T(8,128)(2,1)S(1)} all-gather(bf16[272,256]{1,0:T(8,128)(2,1)S(1)} %shard_map.167), channel_id=3, replica_groups=mesh['y'=4,'core'=2,'zg'=8,'zl'=2,'x'=4] {'y'}, dimensions={0}, use_global_device_ids=true | all-gather | bytes 696320 | tf_op jit(solution)/shard_map/all_gather | solution.py:324
  42.8 1.7 shard_map.168
  44.5 3.3 %all-to-all-start = ((f32[8,1,128]{2,1,0:T(1,128)}), f32[8,1,128]{2,1,0:T(1,128)S(1)}, u32[]{:S(2)}, u32[]{:S(2)}) async-start(f32[8,1,128]{2,1,0:T(1,128)} %bitcast.14), calls=%async_computation | async-start | bytes 8192 | tf_op jit(solution)/shard_map/all_to_all | solution.py:333
  47.9 4.8 %all-to-all-done = f32[8,1,128]{2,1,0:T(1,128)S(1)} async-done(((f32[8,1,128]{2,1,0:T(1,128)}), f32[8,1,128]{2,1,0:T(1,128)S(1)}, u32[]{:S(2)}, u32[]{:S(2)}) %all-to-all-start) | async-done | bytes 4128 | tf_op jit(solution)/shard_map/all_to_all | solution.py:333
  52.7 0.7 shard_map.169
  53.3 31.3 %all-gather.2 = bf16[1024,256]{1,0:T(8,128)(2,1)S(1)} all-gather(bf16[128,256]{1,0:T(8,128)(2,1)S(1)} %shard_map.169), channel_id=4, replica_groups=mesh['y'=4,'core'=2,'zg'=8,'zl'=2,'x'=4] {'zg'}, dimensions={0}, use_global_device_ids=true | all-gather | bytes 589824 | tf_op jit(solution)/shard_map/all_gather | solution.py:337
  84.7 1.9 collective-permute-start
  86.6 2.7 %copy-done.1 = bf16[32,1,2,1,256,128]{5,4,3,2,1,0:T(8,128)(2,1)S(1)} copy-done((bf16[32,1,2,1,256,128]{5,4,3,2,1,0:T(8,128)(2,1)S(1)}, bf16[32,1,2,1,256,128]{5,4,3,2,1,0:T(8,128)(2,1)}, u32[]{:S(2)}) %copy-start.1) | copy-done | bytes 4194328
  89.3 1.0 shard_map.170.refs_3_
  90.3 5.3 %collective-permute-done.refs_1_ = bf16[8,128,256]{2,1,0:T(8,128)(2,1)S(1)} collective-permute-done((bf16[8,128,256]{2,1,0:T(8,128)(2,1)S(1)}, bf16[8,128,256]{2,1,0:T(8,128)(2,1)S(1)}, u32[]{:S(2)}, u32[]{:S(2)}) %collective-permute-start) | collective-permute-done | bytes 524320 | tf_op jit(solution)/shard_map/ppermute | solution.py:270
  95.7 1.0 shard_map.171
  96.7 8.0 %all_to_all.54.parts = f32[4,128,128]{2,1,0:T(8,128)S(1)} all-to-all(f32[4,128,128]{2,1,0:T(8,128)S(1)} %shard_map.171), channel_id=1, replica_groups=mesh['y'=4,'core'=2,'zg'=8,'zl'=2,'x'=4] {'x'}, dimensions={0} | all-to-all | bytes 524288 | tf_op jit(solution)/shard_map/all_to_all | solution.py:340
  104.6 0.6 shard_map.172
  105.3 26.3 %all-gather.4 = bf16[2048,128]{1,0:T(8,128)(2,1)S(1)} all-gather(bf16[128,128]{1,0:T(8,128)(2,1)S(1)} %get-tuple-element.18), channel_id=6, replica_groups=mesh['y'=4,'core'=2,'zg'=8,'zl'=2,'x'=4] {'zg','zl'}, dimensions={0}, use_global_device_ids=true | all-gather | bytes 557056 | tf_op jit(solution)/shard_map/all_gather | solution.py:344
  131.5 2.6 %collective-permute-start.1 = (bf16[16,128,128]{2,1,0:T(8,128)(2,1)S(1)}, bf16[16,128,128]{2,1,0:T(8,128)(2,1)S(1)}, u32[]{:S(2)}, u32[]{:S(2)}) collective-permute-start(bf16[16,128,128]{2,1,0:T(8,128)(2,1)S(1)} %bitcast.49), channel_id=1, source_target_pairs={{0,1},{1,2},{2,3},{3,0},{4,5},{5,6},{6,7},{7,4},{8,9},{9,10},{10,1... | collective-permute-start | bytes 1572872 | tf_op jit(solution)/shard_map/ppermute | solution.py:270
  134.1 3.3 %collective-permute-start.2 = (bf16[16,128,128]{2,1,0:T(8,128)(2,1)S(1)}, bf16[16,128,128]{2,1,0:T(8,128)(2,1)S(1)}, u32[]{:S(2)}, u32[]{:S(2)}) collective-permute-start(bf16[16,128,128]{2,1,0:T(8,128)(2,1)S(1)} %bitcast.50), channel_id=1, source_target_pairs={{0,2},{1,3},{2,0},{3,1},{4,6},{5,7},{6,4},{7,5},{8,10},{9,11},{10,... | collective-permute-start | bytes 1572872 | tf_op jit(solution)/shard_map/ppermute | solution.py:270
  137.4 2.9 %collective-permute-start.3 = (bf16[16,128,128]{2,1,0:T(8,128)(2,1)S(1)}, bf16[16,128,128]{2,1,0:T(8,128)(2,1)S(1)}, u32[]{:S(2)}, u32[]{:S(2)}) collective-permute-start(bf16[16,128,128]{2,1,0:T(8,128)(2,1)S(1)} %bitcast.51), channel_id=1, source_target_pairs={{0,3},{1,0},{2,1},{3,2},{4,7},{5,4},{6,5},{7,6},{8,11},{9,8},{10,9... | collective-permute-start | bytes 1572872 | tf_op jit(solution)/shard_map/ppermute | solution.py:270
  140.6 8.1 %collective-permute-done.1.p1 = bf16[16,128,128]{2,1,0:T(8,128)(2,1)S(1)} collective-permute-done((bf16[16,128,128]{2,1,0:T(8,128)(2,1)S(1)}, bf16[16,128,128]{2,1,0:T(8,128)(2,1)S(1)}, u32[]{:S(2)}, u32[]{:S(2)}) %collective-permute-start.1) | collective-permute-done | bytes 524320 | tf_op jit(solution)/shard_map/ppermute | solution.py:270
  148.7 2.5 %collective-permute-done.3.p3 = bf16[16,128,128]{2,1,0:T(8,128)(2,1)S(1)} collective-permute-done((bf16[16,128,128]{2,1,0:T(8,128)(2,1)S(1)}, bf16[16,128,128]{2,1,0:T(8,128)(2,1)S(1)}, u32[]{:S(2)}, u32[]{:S(2)}) %collective-permute-start.3) | collective-permute-done | bytes 524320 | tf_op jit(solution)/shard_map/ppermute | solution.py:270
  151.2 9.7 %all-gather.11.cloned.1.call-done = bf16[8192,1024]{1,0:T(8,128)(2,1)} async-done(((bf16[1024,1024]{1,0:T(8,128)(2,1)}), bf16[8192,1024]{1,0:T(8,128)(2,1)}) %all-gather.11.cloned.1.call-update) | async-done | bytes 16777232 | tf_op jit(solution)/shard_map/all_gather | solution.py:320
  161.0 10.0 %shard_map.173 = f32[128,128]{1,0:T(8,128)S(1)} custom-call(s32[7]{0:T(128)S(1)} %stack.31.place.refs_0_, bf16[16,128,128]{2,1,0:T(8,128)(2,1)S(1)} %bitcast.52, bf16[16,128,128]{2,1,0:T(8,128)(2,1)S(1)} %collective-permute-done.1.p1, bf16[16,128,128]{2,1,0:T(8,128)(2,1)S(1)} %collective-permute-done.2.p2, bf16[16,128,128]{2,1,0:T(8,128)(2,1)} %copy-done.10, ...), custom_call_target="tpu_custom_call" | custom-call | flops 2147483648 | bytes 18874368 | tf_op jit(solution)/shard_map/pallas_call | solution.py:217
  171.0 29.2 %all_to_all.55 = f32[64,2,128]{2,1,0:T(2,128)S(1)} all-to-all(f32[64,2,128]{2,1,0:T(2,128)S(1)} %bitcast.57), channel_id=1, replica_groups=mesh['y'=4,'core'=2,'zg'=8,'zl'=2,'x'=4] {'zg','zl','x'}, dimensions={0} | all-to-all | bytes 131072 | tf_op jit(solution)/shard_map/all_to_all | solution.py:350
  200.2 1.1 shard_map.174
  201.3 10.4 %all_to_all.56 = f32[8,1,128]{2,1,0:T(1,128)S(1)} all-to-all(f32[8,1,128]{2,1,0:T(1,128)S(1)} %bitcast.68), channel_id=1, replica_groups=mesh['y'=4,'core'=2,'zg'=8,'zl'=2,'x'=4] {'y','core'}, dimensions={0} | all-to-all | bytes 8192 | tf_op jit(solution)/shard_map/all_to_all | solution.py:356
  211.7 0.3 shard_map.175
  212.0 0.5 slice_bitcast_fusion
  (42 shorter events, 0.8 us)
Async XLA Ops:
  7.2 133.2 %copy-start = (s32[1024]{0:T(1024)S(1)}, s32[1024]{0:T(1024)}, u32[]{:S(2)}) copy-start(s32[1024]{0:T(1024)} %param.27) | copy-start | bytes 12292
  7.2 13.8 %copy-start.12 = (f32[128,4]{0,1:T(4,128)S(1)}, f32[128,4]{0,1:T(4,128)}, u32[]{:S(2)}) copy-start(f32[128,4]{0,1:T(4,128)} %param.20) | copy-start | bytes 6148
  7.2 14.0 %copy-start.13 = (f32[4]{0:T(128)S(1)}, f32[4]{0:T(128)}, u32[]{:S(2)}) copy-start(f32[4]{0:T(128)} %param.22) | copy-start | bytes 52
  7.2 15.7 %copy-start.5 = (s32[1024]{0:T(1024)S(1)}, s32[1024]{0:T(1024)}, u32[]{:S(2)}) copy-start(s32[1024]{0:T(1024)} %param.28) | copy-start | bytes 12292
  7.2 15.7 %copy-start.9 = (f32[4]{0:T(128)S(1)}, f32[4]{0:T(128)}, u32[]{:S(2)}) copy-start(f32[4]{0:T(128)} %param.21) | copy-start | bytes 52
  7.2 15.7 %copy-start.4 = (bf16[128,256]{1,0:T(8,128)(2,1)S(1)}, bf16[128,256]{1,0:T(8,128)(2,1)}, u32[]{:S(2)}) copy-start(bf16[128,256]{1,0:T(8,128)(2,1)} %x_ref.1) | copy-start | bytes 196612
  7.2 35.6 %copy-start.3 = (bf16[128,256]{1,0:T(8,128)(2,1)S(1)}, bf16[128,256]{1,0:T(8,128)(2,1)}, u32[]{:S(2)}) copy-start(bf16[128,256]{1,0:T(8,128)(2,1)} %gate.1) | copy-start | bytes 196612
  7.2 79.3 %all-gather.9.cloned.1.call-start = ((), (), s32[]{:S(2)}) async-start(), calls=%async_computation.5 | async-start | bytes 4718592 | tf_op jit(solution)/shard_map/all_gather | solution.py:319
  8.4 39.4 %copy-start.11 = (f32[16384]{0:T(1024)S(1)}, f32[16384]{0:T(1024)}, u32[]{:S(2)}) copy-start(f32[16384]{0:T(1024)} %param.23) | copy-start | bytes 196612
  20.3 140.7 %all-gather.11.cloned.1.call-start = ((), (), s32[]{:S(2)}) async-start(), calls=%async_computation.6 | async-start | bytes 18874368 | tf_op jit(solution)/shard_map/all_gather | solution.py:320
  44.5 8.2 %all-to-all-start = ((f32[8,1,128]{2,1,0:T(1,128)}), f32[8,1,128]{2,1,0:T(1,128)S(1)}, u32[]{:S(2)}, u32[]{:S(2)}) async-start(f32[8,1,128]{2,1,0:T(1,128)} %bitcast.14), calls=%async_computation | async-start | bytes 8192 | tf_op jit(solution)/shard_map/all_to_all | solution.py:333
  84.7 11.0 %collective-permute-start = (bf16[8,128,256]{2,1,0:T(8,128)(2,1)S(1)}, bf16[8,128,256]{2,1,0:T(8,128)(2,1)S(1)}, u32[]{:S(2)}, u32[]{:S(2)}) collective-permute-start(bf16[8,128,256]{2,1,0:T(8,128)(2,1)S(1)} %bitcast.53), channel_id=1, source_target_pairs={{0,4},{4,0},{1,5},{5,1},{2,6},{6,2},{3,7},{7,3},{8,12},{12,8},{9,1... | collective-permute-start | bytes 1572872 | tf_op jit(solution)/shard_map/ppermute | solution.py:270
  86.6 2.7 %copy-start.1 = (bf16[32,1,2,1,256,128]{5,4,3,2,1,0:T(8,128)(2,1)S(1)}, bf16[32,1,2,1,256,128]{5,4,3,2,1,0:T(8,128)(2,1)}, u32[]{:S(2)}) copy-start(bf16[32,1,2,1,256,128]{5,4,3,2,1,0:T(8,128)(2,1)} %all-gather.9.cloned.1.call-done) | copy-start | bytes 12582916
  89.3 6.3 %copy-start.2 = (bf16[32,1,2,1,256,128]{5,4,3,2,1,0:T(8,128)(2,1)S(1)}, bf16[32,1,2,1,256,128]{5,4,3,2,1,0:T(8,128)(2,1)}, u32[]{:S(2)}) copy-start(bf16[32,1,2,1,256,128]{5,4,3,2,1,0:T(8,128)(2,1)} %all-gather.9.cloned.1.call-done) | copy-start | bytes 12582916
  89.3 15.3 %copy-start.7 = (bf16[128,128]{1,0:T(8,128)(2,1)S(1)}, bf16[128,128]{1,0:T(8,128)(2,1)}, u32[]{:S(2)}) copy-start(bf16[128,128]{1,0:T(8,128)(2,1)} %residual.1) | copy-start | bytes 98308
  90.3 70.6 %copy-start.6 = (f32[8192]{0:T(1024)S(1)}, f32[8192]{0:T(1024)}, u32[]{:S(2)}) copy-start(f32[8192]{0:T(1024)} %param.25) | copy-start | bytes 98308
  131.5 17.1 %collective-permute-start.1 = (bf16[16,128,128]{2,1,0:T(8,128)(2,1)S(1)}, bf16[16,128,128]{2,1,0:T(8,128)(2,1)S(1)}, u32[]{:S(2)}, u32[]{:S(2)}) collective-permute-start(bf16[16,128,128]{2,1,0:T(8,128)(2,1)S(1)} %bitcast.49), channel_id=1, source_target_pairs={{0,1},{1,2},{2,3},{3,0},{4,5},{5,6},{6,7},{7,4},{8,9},{9,10},{10,1... | collective-permute-start | bytes 1572872 | tf_op jit(solution)/shard_map/ppermute | solution.py:270
  134.1 14.6 %collective-permute-start.2 = (bf16[16,128,128]{2,1,0:T(8,128)(2,1)S(1)}, bf16[16,128,128]{2,1,0:T(8,128)(2,1)S(1)}, u32[]{:S(2)}, u32[]{:S(2)}) collective-permute-start(bf16[16,128,128]{2,1,0:T(8,128)(2,1)S(1)} %bitcast.50), channel_id=1, source_target_pairs={{0,2},{1,3},{2,0},{3,1},{4,6},{5,7},{6,4},{7,5},{8,10},{9,11},{10,... | collective-permute-start | bytes 1572872 | tf_op jit(solution)/shard_map/ppermute | solution.py:270
  137.4 13.8 %collective-permute-start.3 = (bf16[16,128,128]{2,1,0:T(8,128)(2,1)S(1)}, bf16[16,128,128]{2,1,0:T(8,128)(2,1)S(1)}, u32[]{:S(2)}, u32[]{:S(2)}) collective-permute-start(bf16[16,128,128]{2,1,0:T(8,128)(2,1)S(1)} %bitcast.51), channel_id=1, source_target_pairs={{0,3},{1,0},{2,1},{3,2},{4,7},{5,4},{6,5},{7,6},{8,11},{9,8},{10,9... | collective-permute-start | bytes 1572872 | tf_op jit(solution)/shard_map/ppermute | solution.py:270
  151.2 9.8 %copy-start.10 = (bf16[16,128,128]{2,1,0:T(8,128)(2,1)}, bf16[16,128,128]{2,1,0:T(8,128)(2,1)S(1)}, u32[]{:S(2)}) copy-start(bf16[16,128,128]{2,1,0:T(8,128)(2,1)S(1)} %collective-permute-done.3.p3) | copy-start | bytes 1572868
  161.0 39.2 %copy-start.8 = (s32[1024]{0:T(1024)S(1)}, s32[1024]{0:T(1024)}, u32[]{:S(2)}) copy-start(s32[1024]{0:T(1024)} %param.29) | copy-start | bytes 12292
Sparse Core Ops, SparseCore 0:
  20.4 45.6 all-gather.8
  68.3 92.6 all-gather.10

commit v2 on v1

--- a/solution.py
+++ b/solution.py
@@ -58,7 +58,7 @@
 def scan_kernel(place, seg, step_raw, decay_log, skip, x_ref, b_ref, c_ref, inner, carry, msg):
     row_start = place[0] * ROWS
     boundary = seg.shape[0] * seg.shape[1] - jnp.sum(seg[...])
-    raw = step_raw[...]
+    raw = jnp.concatenate([step_raw[...]] * (ROWS // HEADS), axis=0).T[:, 0:HEADS]
     step = jnp.maximum(raw, 0.0) + jnp.log1p(jnp.exp(-jnp.abs(raw)))
     log_decay = -jnp.exp(decay_log[...]) * step
     share = ROWS // HEADS
@@ -88,7 +88,8 @@
         weight = jnp.where(allowed, jnp.exp(jnp.where(allowed, gap, 0.0)), 0.0)
         part = slice(h * WIDTH, (h + 1) * WIDTH)
         inner[:, part] = dot(scores * weight, scaled[:, part], HIGH)
-    inner[...] += skip[...] * inputs
+    gains = jnp.broadcast_to(skip[...], (ROWS, HEADS))
+    inner[...] += head_columns([gains[:, h : h + 1] for h in range(HEADS)]) * inputs
     carry[...] = jnp.where(seg_rows == seg_before, jnp.exp(wide), 0.0)
     last = wide[ROWS - 1 : ROWS, :]
     to_end = jnp.where(seg_rows == seg_last, jnp.exp(last - wide), 0.0)
@@ -114,7 +115,7 @@
     )
 
 
-def gate_kernel(place, chips, pair, c_ref, inner, carry, gate, out, squares):
+def gate_kernel(place, chips, pair, c_ref, inner, carry, gate, out):
     y, core = (place[1], place[2])
     state = jnp.zeros((STATE, CHANNELS), F32)
     for k in range(NY - 1):
@@ -126,47 +127,41 @@
     )
     ssd = inner[...] + carry[...] * dot(c_ref[...].astype(F32), state, HIGH)
     v = gate[...].astype(F32)
-    gated = (ssd * (v / (1.0 + jnp.exp(-v)))).astype(BF16)
-    out[...] = gated
-    rounded = gated.astype(F32)
-    column = jnp.sum(rounded * rounded, axis=1, keepdims=True)
-    squares[...] = jnp.broadcast_to(column, (ROWS, ROWS)).T[0:8, :]
-
-
-def norm_kernel(place, gated, squares, gain, out):
-    line = jnp.sum(squares[...], axis=0, keepdims=True)
-    scale = lax.rsqrt(jnp.broadcast_to(line, (ROWS, ROWS)).T / 2048.0 + EPS)
-    wide = jnp.concatenate([scale] * (CHANNELS // ROWS), axis=1)
-    out[...] = (gated[...].astype(F32) * wide * gain[pl.ds(place[5], 1), :]).astype(BF16)
-
-
-def project_kernel(other, place, rows, weight, *rest):
-    before, out = rest if other else (None,) + rest
-    side = lax.rem(place[6] + other, NL)
-    total = before[...] if other else jnp.zeros((ROWS, NX * ROWS), F32)
+    out[...] = (ssd * (v / (1.0 + jnp.exp(-v)))).astype(BF16)
+
+
+def square_kernel(rows, out):
+    lane = lax.broadcasted_iota(jnp.int32, (ROWS, ROWS), 1)
+    table = jnp.zeros((ROWS, ROWS), F32)
     for g in range(NG):
-        total = total + dot(
-            rows[g], jnp.concatenate([weight[g, k, side] for k in range(NX)], axis=1)
-        )
-    if other:
-        for k in range(NX):
-            out[k] = total[:, k * ROWS : (k + 1) * ROWS]
-    else:
-        out[...] = total
-
-
-def project(place, rows, weight, before=None):
-    other = 0 if before is None else 1
-    return pl.pallas_call(
-        lambda *refs: project_kernel(other, *refs),
-        out_shape=jax.ShapeDtypeStruct((NX, ROWS, ROWS) if other else (ROWS, NX * ROWS), F32),
-        in_specs=[smem()] + [vmem()] * (2 + other),
-        out_specs=vmem(),
-        cost_estimate=pl.CostEstimate(
-            flops=2 * ROWS * NG * CHANNELS * NX * ROWS, bytes_accessed=1 << 22, transcendentals=0
-        ),
-        compiler_params=pltpu.CompilerParams(vmem_limit_bytes=32 * 1024 * 1024),
-    )(place, rows, weight, *([before] if other else []))
+        v = rows[g].astype(F32)
+        table = jnp.where(lane == g, jnp.sum(v * v, axis=1, keepdims=True), table)
+    line = table.T[0:NG, :]
+    for k in range(NL * NX):
+        out[k] = line
+
+
+def project_kernel(place, mine, paired, squares, gain, same, other, out):
+    side = place[6]
+    total = squares[0]
+    for k in range(1, NL * NX):
+        total = total + squares[k]
+    scale = lax.rsqrt(total / 2048.0 + EPS)
+    scale = jnp.concatenate([scale] * (ROWS // NG), axis=0).T
+    result = jnp.zeros((ROWS, NX * ROWS), F32)
+    lane = lax.broadcasted_iota(jnp.int32, (ROWS, ROWS), 1)
+    for c, weight in enumerate((same, other)):
+        core = lax.rem(place[2] + c, NC)
+        for j in range(NY):
+            g = j * NC + core
+            column = jnp.sum(jnp.where(lane == g, scale, 0.0), axis=1, keepdims=True)
+            for rows, half in ((mine, side), (paired, 1 - side)):
+                line = (NL * g + half) * NX + place[4]
+                normed = (rows[g].astype(F32) * column * gain[pl.ds(line, 1), :]).astype(BF16)
+                block = jnp.concatenate([weight[j, k, half] for k in range(NX)], axis=1)
+                result = result + dot(normed, block)
+    for k in range(NX):
+        out[k] = result[:, k * ROWS : (k + 1) * ROWS]
 
 
 def residual_kernel(parts, residual, mixer_out, summed):
@@ -175,63 +170,93 @@
     summed[...] = (residual[...].astype(F32) + mixed.astype(F32)).astype(BF16)
 
 
-def head_kernel(place, p0, p1, p2, p3, gain, wanted, weight, out, total, squares):
-    s = pl.program_id(0)
-
-    @pl.when(s == 0)
-    def _():
-        total[...] = jnp.zeros_like(total)
-        squares[...] = jnp.zeros_like(squares)
-
-    square = jnp.zeros((ROWS, ROWS), F32)
+def scaled_blocks(parts, sources, gain, g, square):
+    blocks = []
+    for part, source in zip(parts, sources):
+        for half in range(NL):
+            v = part[NL * g + half].astype(F32)
+            square = square + v * v
+            blocks.append((v * gain[NL * g + half, source]).astype(BF16))
+    return jnp.concatenate(blocks, axis=1), square
+
+
+def own_kernel(place, part, gain, weight, total, squares, later, held, arrived):
+    copies = []
+    for k in range(NX):
+        source = lax.rem(place[4] + NX - k, NX)
+        for g in range(NG):
+            for half in range(NL):
+                target = later.at[g, k - 1, half] if k else held.at[g, half]
+                copies.append(
+                    pltpu.make_async_copy(
+                        weight.at[g, half, source], target, arrived.at[k, g, half]
+                    )
+                )
+                copies[-1].start()
+    result = jnp.zeros(total.shape, F32)
+    square = jnp.zeros(squares.shape, F32)
+    for g in range(NG):
+        rows, square = scaled_blocks([part], [place[4]], gain, g, square)
+        for half in range(NL):
+            copies[NL * g + half].wait()
+        result = result + dot(rows, jnp.concatenate([held[g, h] for h in range(NL)], axis=0))
+    total[...] = result
+    squares[...] = square
+    for copy in copies[NG * NL :]:
+        copy.wait()
+
+
+def rest_kernel(place, p1, p2, p3, gain, weight, total, squares, wanted, out):
+    parts = (p1, p2, p3)
+    sources = [lax.rem(place[4] + NX - k, NX) for k in range(1, NX)]
     result = total[...]
-    for k, part in enumerate((p0, p1, p2, p3)):
-        source = lax.rem(place[4] + NX - k, NX)
-        blocks = []
-        for half in range(NL):
-            v = part[half].astype(F32)
-            square = square + v * v
-            blocks.append((v * gain[half, source]).astype(BF16))
-        pieces = [weight[0, half, source] for half in range(NL)]
-        result = result + dot(
-            jnp.concatenate(blocks, axis=1), jnp.concatenate(pieces, axis=0)
-        )
-    total[...] = result
-    squares[...] += square
-
-    @pl.when(s == pl.num_programs(0) - 1)
-    def _():
-        mean = jnp.sum(squares[...], axis=1, keepdims=True) / 8192.0
-        logits = total[...] * lax.rsqrt(mean + EPS)
-        top = jnp.max(logits, axis=1, keepdims=True)
-        mass = jnp.sum(jnp.exp(logits - top), axis=1, keepdims=True)
-        first = place[5] * logits.shape[1]
-        vocab = first + lax.broadcasted_iota(jnp.int32, logits.shape, 1)
-        picked = jnp.sum(jnp.where(vocab == wanted[...], logits, 0.0), axis=1, keepdims=True)
-        lane = lax.broadcasted_iota(jnp.int32, (ROWS, ROWS), 1)
-        out[...] = jnp.where(lane % 2 == 0, top + jnp.log(mass), picked).T
-
-
-def head(place, parts, gain, wanted, weight):
+    square = squares[...]
+    for g in range(NG):
+        rows, square = scaled_blocks(parts, sources, gain, g, square)
+        pieces = [weight[g, k, half] for k in range(NX - 1) for half in range(NL)]
+        result = result + dot(rows, jnp.concatenate(pieces, axis=0))
+    mean = jnp.sum(square, axis=1, keepdims=True) / 8192.0
+    logits = result * lax.rsqrt(mean + EPS)
+    top = jnp.max(logits, axis=1, keepdims=True)
+    mass = jnp.sum(jnp.exp(logits - top), axis=1, keepdims=True)
+    begin = place[5] * logits.shape[1]
+    vocab = begin + lax.broadcasted_iota(jnp.int32, logits.shape, 1)
+    picked = jnp.sum(jnp.where(vocab == wanted[...], logits, 0.0), axis=1, keepdims=True)
+    lane = lax.broadcasted_iota(jnp.int32, (ROWS, ROWS), 1)
+    out[...] = jnp.where(lane % 2 == 0, top + jnp.log(mass), picked).T
+
+
+def head(place, parts, gain, weight, wanted):
     columns = weight.shape[-1]
+    square = jax.ShapeDtypeStruct((ROWS, ROWS), F32)
+    cost = pl.CostEstimate(
+        flops=2 * ROWS * NZ * ROWS * columns, bytes_accessed=1 << 24, transcendentals=0
+    )
+    params = pltpu.CompilerParams(vmem_limit_bytes=32 * 1024 * 1024)
+    total, squares, later = pl.pallas_call(
+        own_kernel,
+        out_shape=(
+            jax.ShapeDtypeStruct((ROWS, columns), F32),
+            square,
+            jax.ShapeDtypeStruct((NG, NX - 1, NL, ROWS, columns), BF16),
+        ),
+        in_specs=[smem(), vmem(), vmem(), pl.BlockSpec(memory_space=pl.ANY)],
+        out_specs=[vmem()] * 3,
+        scratch_shapes=[
+            pltpu.VMEM((NG, NL, ROWS, columns), BF16),
+            pltpu.SemaphoreType.DMA((NX, NG, NL)),
+        ],
+        cost_estimate=cost,
+        compiler_params=params,
+    )(place, parts[0], gain, weight)
     return pl.pallas_call(
-        head_kernel,
-        grid=(NG,),
-        out_shape=jax.ShapeDtypeStruct((ROWS, ROWS), F32),
-        in_specs=[smem()]
-        + [pl.BlockSpec((NL, ROWS, ROWS), lambda s: (s, 0, 0))] * NX
-        + [
-            pl.BlockSpec((NL, NX, 1, ROWS), lambda s: (s, 0, 0, 0)),
-            pl.BlockSpec((ROWS, 1), lambda s: (0, 0)),
-            pl.BlockSpec((1, NL, NX, ROWS, columns), lambda s: (s, 0, 0, 0, 0)),
-        ],
-        out_specs=pl.BlockSpec((ROWS, ROWS), lambda s: (0, 0)),
-        scratch_shapes=[pltpu.VMEM((ROWS, columns), F32), pltpu.VMEM((ROWS, ROWS), F32)],
-        cost_estimate=pl.CostEstimate(
-            flops=2 * ROWS * NX * NZ * ROWS * columns, bytes_accessed=18 << 20, transcendentals=0
-        ),
-        compiler_params=pltpu.CompilerParams(vmem_limit_bytes=52 * 1024 * 1024),
-    )(place, *parts, gain, wanted, weight)
+        rest_kernel,
+        out_shape=square,
+        in_specs=[smem()] + [vmem()] * (NX + 4),
+        out_specs=vmem(),
+        cost_estimate=cost,
+        compiler_params=params,
+    )(place, *parts[1:], gain, later, total, squares, wanted)
 
 
 def token_kernel(place, stats, seg, mask, logp, sums):
@@ -297,6 +322,9 @@
     b_rows = lax.dynamic_index_in_dim(b_proj, group, 1, keepdims=False)
     c_rows = lax.dynamic_index_in_dim(c_proj, group, 1, keepdims=False)
 
+    rows = out_weight.reshape(1, NL, NX, CHANNELS, ROWS).transpose(0, 2, 1, 3, 4)
+    rows = jnp.broadcast_to(rows, (NY, *rows.shape[1:])).reshape(NY * NX, NL, CHANNELS, ROWS)
+    rows, b_rows = lax.optimization_barrier((rows, b_rows))
     inner, carry, msg = call(
         scan_kernel,
         (
@@ -308,36 +336,36 @@
     )(
         place,
         seg,
-        step_raw,
+        step_raw.T,
         decay_log.reshape(1, HEADS),
-        jnp.repeat(skip_gain, WIDTH).reshape(1, CHANNELS),
+        skip_gain.reshape(1, HEADS),
         ssm_input,
         b_rows,
         c_rows,
     )
-    turned = lax.all_to_all(out_weight.reshape(NL, NX, CHANNELS, ROWS), "x", 1, 0)
-    out_rows = lax.all_gather(turned, SEQ)
-    head_rows = lax.all_gather(head_weight, SEQ)
-
     pair = lax.all_gather(msg, "core")
     chip = call(chip_kernel, jax.ShapeDtypeStruct((MSG, CHANNELS), BF16), [vmem()])(pair)
     chips = lax.all_gather(chip, "y")
-    gated, squares = call(
-        gate_kernel,
-        (
-            jax.ShapeDtypeStruct((ROWS, CHANNELS), BF16),
-            jax.ShapeDtypeStruct((8, ROWS), F32),
-        ),
-        [smem()] + [vmem()] * 6,
+    gated = call(
+        gate_kernel, jax.ShapeDtypeStruct((ROWS, CHANNELS), BF16), [smem()] + [vmem()] * 6
     )(place, chips, pair, c_rows, inner, carry, gate_input)
-    squares = lax.all_to_all(squares, ("zl", "x"), 0, 0, tiled=True)
-    normed = call(
-        norm_kernel, jax.ShapeDtypeStruct((ROWS, CHANNELS), BF16), [smem()] + [vmem()] * 3
-    )(place, gated, squares, mixer_gain.reshape(-1, CHANNELS))
-    same = lax.all_gather(normed, "zg")
-    other = shifted(same, "zl", 1)
-    total = project(place, same, out_rows)
-    parts = lax.all_to_all(project(place, other, out_rows, total), "x", 0, 0)
+    rows, weight, gated = lax.optimization_barrier((rows, head_weight, gated))
+    same = lax.all_to_all(rows, ("y", "x"), 0, 0).reshape(NY, NX, NL, CHANNELS, ROWS)
+    head_rows = lax.all_gather(weight, SEQ)
+    mine = lax.all_gather(gated, "zg")
+    odd = range(1, NZ, NL)
+    swaps = [(i, (i + 1) % NZ) for i in odd] + [((i + 1) % NZ, i) for i in odd]
+    same, mine = lax.optimization_barrier((same, mine))
+    other = shifted(same, "core", 1)
+    paired = lax.ppermute(mine, ("zg", "zl"), swaps)
+    squares = call(
+        square_kernel, jax.ShapeDtypeStruct((NL * NX, NG, ROWS), F32), [vmem()]
+    )(mine)
+    squares = lax.all_to_all(squares, ("zl", "x"), 0, 0)
+    parts = call(
+        project_kernel, jax.ShapeDtypeStruct((NX, ROWS, ROWS), F32), [smem()] + [vmem()] * 6
+    )(place, mine, paired, squares, mixer_gain.reshape(-1, CHANNELS), same, other)
+    parts = lax.all_to_all(parts, "x", 0, 0)
     half = jax.ShapeDtypeStruct((ROWS, ROWS), BF16)
     mixer_out, summed = call(residual_kernel, (half, half), [vmem()] * 2)(parts, residual_in)
 
@@ -346,7 +374,7 @@
     wanted = lax.dynamic_slice_in_dim(targets, seq * ROWS, ROWS).reshape(ROWS, 1)
     gains = final_gain.reshape(NZ, NX, 1, ROWS)
     matrix = head_rows.reshape(NG, NL, NX, ROWS, -1)
-    stats = head(place, features, gains, wanted, matrix)
+    stats = head(place, features, gains, matrix, wanted)
     stats = lax.all_to_all(stats, MP, 0, 0, tiled=True)
     logp, sums = call(
         token_kernel,

time: 220 us -> 211 us (0.959)
  starting transfers between devices: 14.1 us -> 30.1 us
  waiting for transfers between devices: 31.3 us -> 19.2 us
  blocking collectives: 135 us -> 124 us
    all_to_all x2 -> x1, blocking collectives: 19.8 us -> 9.69 us  [local(): parts = lax.all_to_all(parts, 'x', 0, 0)]
    all_gather x2 -> x1, waiting for transfers between devices: 9.77 us -> 0.01 us  [local(): head_rows = lax.all_gather(weight, SEQ)]
    ppermute x4, starting transfers between devices: 10.7 us -> 18.4 us  [shifted(): return lax.ppermute(part, axis, [(i, (i + k) % n) for i in range(n)])]
    all_to_all x1 -> x2, starting transfers between devices: 3.31 us -> 8.12 us  [the longest x1 4.26 us: local(): squares = lax.all_to_all(squares, ('zl', 'x'), 0, 0)]
    ppermute x4, waiting for transfers between devices: 16 us -> 11.2 us  [shifted(): return lax.ppermute(part, axis, [(i, (i + k) % n) for i in range(n)])]
    all_to_all x1, blocking collectives: 29.2 us -> 25.1 us  [local(): stats = lax.all_to_all(stats, MP, 0, 0, tiled=True)]
    ppermute x0 -> x1, starting transfers between devices: none -> 3.54 us  [local(): paired = lax.ppermute(mine, ('zg', 'zl'), swaps)]
    ppermute x0 -> x1, waiting for transfers between devices: none -> 2.96 us  [local(): paired = lax.ppermute(mine, ('zg', 'zl'), swaps)]
  transfers between devices with their start and end apart: 7 -> 8, of which waited for: 5 -> 4; matrix products, arithmetic and copies ran while one was open for 1% -> 0% of each run, Pallas kernels for 3% -> 5%
where the time goes in v2:
time: 211 us
  blocking collectives  124 us (59%)
  starting transfers between devices  30.1 us (14%)
  waiting for transfers between devices  19.2 us (9%)
  Pallas kernels  17.8 us (8%)
  between operations  14.3 us (7%)
  local copies, waits for them, and re-layouts  5.3 us (3%)
    all_gather x1, blocking collectives, local(): mine = lax.all_gather(gated, 'zg')  31.2 us
    all_gather x1, blocking collectives, local(): column = lax.all_gather(summed, ('zg', 'zl'))  26.3 us
    all_to_all x1, blocking collectives, local(): stats = lax.all_to_all(stats, MP, 0, 0, tiled=True)  25.1 us
    ppermute x4, starting transfers between devices, shifted(): return lax.ppermute(part, axis, [(i, (i + k) % n) for i in range(n)])  18.4 us
    all_to_all x1, blocking collectives, local(): sums = lax.all_to_all(sums, SEQ, 0, 0, tiled=True)  12.9 us
    ppermute x4, waiting for transfers between devices, shifted(): return lax.ppermute(part, axis, [(i, (i + k) % n) for i in range(n)])  11.2 us
    all_gather x1, blocking collectives, local(): chips = lax.all_gather(chip, 'y')  9.96 us
    all_to_all x1, blocking collectives, local(): parts = lax.all_to_all(parts, 'x', 0, 0)  9.69 us
  transfers between devices with their start and end apart: 8, of which 4 were waited for; matrix products, arithmetic and copies ran while one was open for 0% of the time, Pallas kernels for 5%

profile of v2, /device:TPU:1, one launch (start us, length us, event | category | flops | bytes accessed | tf_op | source)
XLA Modules:
  0.0 210.7 jit_solution(8842401085227220307)
XLA Ops:
  7.2 1.5 constant_dynamic-slice_fusion
  8.8 1.1 copy.24
  9.9 1.8 broadcast_in_dim.8
  11.9 1.8 shard_map.166
  13.7 8.7 %all-gather = f32[528,256]{1,0:T(8,128)S(1)} all-gather(f32[264,256]{1,0:T(8,128)S(1)} %get-tuple-element.22), channel_id=2, replica_groups=mesh['y'=4,'core'=2,'zg'=8,'zl'=2,'x'=4] {'core'}, dimensions={0}, use_global_device_ids=true | all-gather | bytes 811008 | tf_op jit(solution)/shard_map/all_gather | solution.py:346
  22.4 10.0 %all-gather.1 = bf16[1088,256]{1,0:T(8,128)(2,1)S(1)} all-gather(bf16[272,256]{1,0:T(8,128)(2,1)S(1)} %shard_map.167), channel_id=3, replica_groups=mesh['y'=4,'core'=2,'zg'=8,'zl'=2,'x'=4] {'y'}, dimensions={0}, use_global_device_ids=true | all-gather | bytes 696320 | tf_op jit(solution)/shard_map/all_gather | solution.py:348
  32.4 0.9 shard_map.168
  33.3 3.9 %all-to-all-start = ((bf16[16,2,256,128]{3,2,1,0:T(8,128)(2,1)}), bf16[16,2,256,128]{3,2,1,0:T(8,128)(2,1)S(1)}, u32[]{:S(2)}, u32[]{:S(2)}) async-start(bf16[16,2,256,128]{3,2,1,0:T(8,128)(2,1)} %bitcast.72), calls=%async_computation | async-start | bytes 4194304 | tf_op jit(solution)/shard_map/all_to_all | solution.py:353
  37.2 31.2 %all-gather.2 = bf16[1024,256]{1,0:T(8,128)(2,1)S(1)} all-gather(bf16[128,256]{1,0:T(8,128)(2,1)S(1)} %shard_map.168), channel_id=4, replica_groups=mesh['y'=4,'core'=2,'zg'=8,'zl'=2,'x'=4] {'zg'}, dimensions={0}, use_global_device_ids=true | all-gather | bytes 589824 | tf_op jit(solution)/shard_map/all_gather | solution.py:355
  68.4 9.7 %collective-permute-start.1 = (bf16[4,4,2,256,128]{4,3,2,1,0:T(8,128)(2,1)S(1)}, bf16[4,4,2,256,128]{4,3,2,1,0:T(8,128)(2,1)}, u32[]{:S(2)}, u32[]{:S(2)}) collective-permute-start(bf16[4,4,2,256,128]{4,3,2,1,0:T(8,128)(2,1)S(1)} %bitcast.42), channel_id=1, source_target_pairs={{0,64},{64,0},{1,65},{65,1},{2,66},{66,2},{3,67},{67,3},{4,68},{68... | collective-permute-start | bytes 6291464 | tf_op jit(solution)/shard_map/ppermute | solution.py:295
  78.1 3.5 %collective-permute-start = (bf16[8,128,256]{2,1,0:T(8,128)(2,1)S(1)}, bf16[8,128,256]{2,1,0:T(8,128)(2,1)S(1)}, u32[]{:S(2)}, u32[]{:S(2)}) collective-permute-start(bf16[8,128,256]{2,1,0:T(8,128)(2,1)S(1)} %bitcast.46), channel_id=1, source_target_pairs={{4,8},{12,16},{20,24},{28,32},{36,40},{44,48},{52,56},{60,0},{8,4}... | collective-permute-start | bytes 1572872 | tf_op jit(solution)/shard_map/ppermute | solution.py:360
  81.7 0.9 shard_map.169
  82.5 4.3 %all-to-all-start.1 = ((f32[8,8,128]{2,1,0:T(8,128)}), f32[8,8,128]{2,1,0:T(8,128)S(1)}, u32[]{:S(2)}, u32[]{:S(2)}) async-start(f32[8,8,128]{2,1,0:T(8,128)} %shard_map.169), calls=%async_computation.1 | async-start | bytes 65536 | tf_op jit(solution)/shard_map/all_to_all | solution.py:364
  86.9 5.1 %all-to-all-done.1.squares = f32[8,8,128]{2,1,0:T(8,128)S(1)} async-done(((f32[8,8,128]{2,1,0:T(8,128)}), f32[8,8,128]{2,1,0:T(8,128)S(1)}, u32[]{:S(2)}, u32[]{:S(2)}) %all-to-all-start.1) | async-done | bytes 32800 | tf_op jit(solution)/shard_map/all_to_all | solution.py:364
  91.9 3.0 %collective-permute-done.paired = bf16[8,128,256]{2,1,0:T(8,128)(2,1)S(1)} collective-permute-done((bf16[8,128,256]{2,1,0:T(8,128)(2,1)S(1)}, bf16[8,128,256]{2,1,0:T(8,128)(2,1)S(1)}, u32[]{:S(2)}, u32[]{:S(2)}) %collective-permute-start) | collective-permute-done | bytes 524320 | tf_op jit(solution)/shard_map/ppermute | solution.py:360
  94.9 2.5 %shard_map.170 = f32[4,128,128]{2,1,0:T(8,128)S(1)} custom-call(s32[7]{0:T(128)S(1)} %stack.31.place, bf16[8,128,256]{2,1,0:T(8,128)(2,1)S(1)} %bitcast.48, bf16[8,128,256]{2,1,0:T(8,128)(2,1)S(1)} %collective-permute-done.paired, f32[8,8,128]{2,1,0:T(8,128)S(1)} %all-to-all-done.1.squares, f32[64,256]{1,0:T(8,128)S(1)} %reshape.52.gain, ...), custom_call_target="tpu_custom_call" | custom-call | tf_op jit(solution)/shard_map/pallas_call | solution.py:365
  97.4 9.7 %all_to_all.37.parts = f32[4,128,128]{2,1,0:T(8,128)S(1)} all-to-all(f32[4,128,128]{2,1,0:T(8,128)S(1)} %shard_map.170), channel_id=1, replica_groups=mesh['y'=4,'core'=2,'zg'=8,'zl'=2,'x'=4] {'x'}, dimensions={0} | all-to-all | bytes 524288 | tf_op jit(solution)/shard_map/all_to_all | solution.py:368
  107.1 0.6 shard_map.171
  107.7 26.3 %all-gather.3 = bf16[2048,128]{1,0:T(8,128)(2,1)S(1)} all-gather(bf16[128,128]{1,0:T(8,128)(2,1)S(1)} %get-tuple-element.30), channel_id=5, replica_groups=mesh['y'=4,'core'=2,'zg'=8,'zl'=2,'x'=4] {'zg','zl'}, dimensions={0}, use_global_device_ids=true | all-gather | bytes 557056 | tf_op jit(solution)/shard_map/all_gather | solution.py:372
  134.1 2.5 %collective-permute-start.2 = (bf16[16,128,128]{2,1,0:T(8,128)(2,1)S(1)}, bf16[16,128,128]{2,1,0:T(8,128)(2,1)S(1)}, u32[]{:S(2)}, u32[]{:S(2)}) collective-permute-start(bf16[16,128,128]{2,1,0:T(8,128)(2,1)S(1)} %bitcast.50), channel_id=1, source_target_pairs={{0,1},{1,2},{2,3},{3,0},{4,5},{5,6},{6,7},{7,4},{8,9},{9,10},{10,1... | collective-permute-start | bytes 1572872 | tf_op jit(solution)/shard_map/ppermute | solution.py:295
  136.6 3.3 %collective-permute-start.3 = (bf16[16,128,128]{2,1,0:T(8,128)(2,1)S(1)}, bf16[16,128,128]{2,1,0:T(8,128)(2,1)S(1)}, u32[]{:S(2)}, u32[]{:S(2)}) collective-permute-start(bf16[16,128,128]{2,1,0:T(8,128)(2,1)S(1)} %bitcast.51), channel_id=1, source_target_pairs={{0,2},{1,3},{2,0},{3,1},{4,6},{5,7},{6,4},{7,5},{8,10},{9,11},{10,... | collective-permute-start | bytes 1572872 | tf_op jit(solution)/shard_map/ppermute | solution.py:295
  139.9 2.9 %collective-permute-start.4 = (bf16[16,128,128]{2,1,0:T(8,128)(2,1)S(1)}, bf16[16,128,128]{2,1,0:T(8,128)(2,1)S(1)}, u32[]{:S(2)}, u32[]{:S(2)}) collective-permute-start(bf16[16,128,128]{2,1,0:T(8,128)(2,1)S(1)} %bitcast.52), channel_id=1, source_target_pairs={{0,3},{1,0},{2,1},{3,2},{4,7},{5,4},{6,5},{7,6},{8,11},{9,8},{10,9... | collective-permute-start | bytes 1572872 | tf_op jit(solution)/shard_map/ppermute | solution.py:295
  142.9 0.1 copy.27.wanted
  143.1 6.9 %shard_map.172 = (f32[128,1024]{1,0:T(8,128)S(1)}, f32[128,128]{1,0:T(8,128)S(1)}, bf16[8,3,2,128,1024]{4,3,2,1,0:T(8,128)(2,1)S(1)}) custom-call(s32[7]{0:T(128)S(1)} %stack.31.place, bf16[16,128,128]{2,1,0:T(8,128)(2,1)S(1)} %bitcast.53, f32[16,4,1,128]{3,2,1,0:T(1,128)S(1)} %bitcast.59, bf16[8,2,4,128,1024]{4,3,2,1,0:T(8,128)(2,1)} %bitcast.71), custom_call_target="tpu_custom_call" | custom-call | flops 536870912 | bytes 16777216 | tf_op jit(solution)/shard_map/pallas_call | solution.py:236
  150.0 4.5 %collective-permute-done.3.p2 = bf16[16,128,128]{2,1,0:T(8,128)(2,1)S(1)} collective-permute-done((bf16[16,128,128]{2,1,0:T(8,128)(2,1)S(1)}, bf16[16,128,128]{2,1,0:T(8,128)(2,1)S(1)}, u32[]{:S(2)}, u32[]{:S(2)}) %collective-permute-start.3) | collective-permute-done | bytes 524320 | tf_op jit(solution)/shard_map/ppermute | solution.py:295
  154.5 6.7 %collective-permute-done.4.p3 = bf16[16,128,128]{2,1,0:T(8,128)(2,1)S(1)} collective-permute-done((bf16[16,128,128]{2,1,0:T(8,128)(2,1)S(1)}, bf16[16,128,128]{2,1,0:T(8,128)(2,1)S(1)}, u32[]{:S(2)}, u32[]{:S(2)}) %collective-permute-start.4) | collective-permute-done | bytes 524320 | tf_op jit(solution)/shard_map/ppermute | solution.py:295
  161.1 2.8 %shard_map.173 = f32[128,128]{1,0:T(8,128)S(1)} custom-call(s32[7]{0:T(128)S(1)} %stack.31.place, bf16[16,128,128]{2,1,0:T(8,128)(2,1)S(1)} %collective-permute-done.2.p1, bf16[16,128,128]{2,1,0:T(8,128)(2,1)S(1)} %collective-permute-done.3.p2, bf16[16,128,128]{2,1,0:T(8,128)(2,1)S(1)} %collective-permute-done.4.p3, f32[16,4,1,128]{3,2,1,0:T(1,128)S(1)} %bitcast.60, ...), custom_call_target="tpu_custom_call" | custom-call | flops 536870912 | bytes 16777216 | tf_op jit(solution)/shard_map/pallas_call | solution.py:252
  163.9 25.1 %all_to_all.38 = f32[64,2,128]{2,1,0:T(2,128)S(1)} all-to-all(f32[64,2,128]{2,1,0:T(2,128)S(1)} %bitcast.56), channel_id=1, replica_groups=mesh['y'=4,'core'=2,'zg'=8,'zl'=2,'x'=4] {'zg','zl','x'}, dimensions={0} | all-to-all | bytes 131072 | tf_op jit(solution)/shard_map/all_to_all | solution.py:378
  189.0 1.1 shard_map.174
  190.1 12.9 %all_to_all.39 = f32[8,1,128]{2,1,0:T(1,128)S(1)} all-to-all(f32[8,1,128]{2,1,0:T(1,128)S(1)} %bitcast.67), channel_id=1, replica_groups=mesh['y'=4,'core'=2,'zg'=8,'zl'=2,'x'=4] {'y','core'}, dimensions={0} | all-to-all | bytes 8192 | tf_op jit(solution)/shard_map/all_to_all | solution.py:384
  203.0 0.3 shard_map.175
  203.3 0.5 slice_bitcast_fusion
  (34 shorter events, 0.4 us)
Async XLA Ops:
  7.2 135.7 %copy-start = (s32[1024]{0:T(1024)S(1)}, s32[1024]{0:T(1024)}, u32[]{:S(2)}) copy-start(s32[1024]{0:T(1024)} %param.27) | copy-start | bytes 12292
  7.2 135.9 %all-gather.7.cloned.1.call-start = ((), (), s32[]{:S(2)}) async-start(), calls=%async_computation.5 | async-start | bytes 18874368 | tf_op jit(solution)/shard_map/all_gather | solution.py:354
  8.7 3.1 %copy-start.2 = (bf16[128,256]{1,0:T(8,128)(2,1)S(1)}, bf16[128,256]{1,0:T(8,128)(2,1)}, u32[]{:S(2)}) copy-start(bf16[128,256]{1,0:T(8,128)(2,1)} %x_ref.1) | copy-start | bytes 196612
  8.7 3.1 %copy-start.4 = (s32[1024]{0:T(1024)S(1)}, s32[1024]{0:T(1024)}, u32[]{:S(2)}) copy-start(s32[1024]{0:T(1024)} %param.28) | copy-start | bytes 12292
  8.7 3.1 %copy-start.7 = (f32[128,4]{0,1:T(4,128)S(1)}, f32[128,4]{0,1:T(4,128)}, u32[]{:S(2)}) copy-start(f32[128,4]{0,1:T(4,128)} %param.20) | copy-start | bytes 6148
  8.8 3.1 %copy-start.8 = (f32[4]{0:T(128)S(1)}, f32[4]{0:T(128)}, u32[]{:S(2)}) copy-start(f32[4]{0:T(128)} %param.21) | copy-start | bytes 52
  8.8 3.1 %copy-start.9 = (f32[4]{0:T(128)S(1)}, f32[4]{0:T(128)}, u32[]{:S(2)}) copy-start(f32[4]{0:T(128)} %param.22) | copy-start | bytes 52
  9.9 22.5 %copy-start.3 = (bf16[128,256]{1,0:T(8,128)(2,1)S(1)}, bf16[128,256]{1,0:T(8,128)(2,1)}, u32[]{:S(2)}) copy-start(bf16[128,256]{1,0:T(8,128)(2,1)} %gate.1) | copy-start | bytes 196612
  33.3 53.5 %copy-start.10 = (f32[16384]{0:T(1024)S(1)}, f32[16384]{0:T(1024)}, u32[]{:S(2)}) copy-start(f32[16384]{0:T(1024)} %param.23) | copy-start | bytes 196612
  33.3 35.1 %all-to-all-start = ((bf16[16,2,256,128]{3,2,1,0:T(8,128)(2,1)}), bf16[16,2,256,128]{3,2,1,0:T(8,128)(2,1)S(1)}, u32[]{:S(2)}, u32[]{:S(2)}) async-start(bf16[16,2,256,128]{3,2,1,0:T(8,128)(2,1)} %bitcast.72), calls=%async_computation | async-start | bytes 4194304 | tf_op jit(solution)/shard_map/all_to_all | solution.py:353
  68.4 26.4 %collective-permute-start.1 = (bf16[4,4,2,256,128]{4,3,2,1,0:T(8,128)(2,1)S(1)}, bf16[4,4,2,256,128]{4,3,2,1,0:T(8,128)(2,1)}, u32[]{:S(2)}, u32[]{:S(2)}) collective-permute-start(bf16[4,4,2,256,128]{4,3,2,1,0:T(8,128)(2,1)S(1)} %bitcast.42), channel_id=1, source_target_pairs={{0,64},{64,0},{1,65},{65,1},{2,66},{66,2},{3,67},{67,3},{4,68},{68... | collective-permute-start | bytes 6291464 | tf_op jit(solution)/shard_map/ppermute | solution.py:295
  78.1 16.8 %collective-permute-start = (bf16[8,128,256]{2,1,0:T(8,128)(2,1)S(1)}, bf16[8,128,256]{2,1,0:T(8,128)(2,1)S(1)}, u32[]{:S(2)}, u32[]{:S(2)}) collective-permute-start(bf16[8,128,256]{2,1,0:T(8,128)(2,1)S(1)} %bitcast.46), channel_id=1, source_target_pairs={{4,8},{12,16},{20,24},{28,32},{36,40},{44,48},{52,56},{60,0},{8,4}... | collective-permute-start | bytes 1572872 | tf_op jit(solution)/shard_map/ppermute | solution.py:360
  82.5 9.4 %all-to-all-start.1 = ((f32[8,8,128]{2,1,0:T(8,128)}), f32[8,8,128]{2,1,0:T(8,128)S(1)}, u32[]{:S(2)}, u32[]{:S(2)}) async-start(f32[8,8,128]{2,1,0:T(8,128)} %shard_map.169), calls=%async_computation.1 | async-start | bytes 65536 | tf_op jit(solution)/shard_map/all_to_all | solution.py:364
  86.8 20.3 %copy-start.5 = (bf16[128,128]{1,0:T(8,128)(2,1)S(1)}, bf16[128,128]{1,0:T(8,128)(2,1)}, u32[]{:S(2)}) copy-start(bf16[128,128]{1,0:T(8,128)(2,1)} %residual.1) | copy-start | bytes 98308
  86.8 56.2 %copy-start.1 = (f32[8192]{0:T(1024)S(1)}, f32[8192]{0:T(1024)}, u32[]{:S(2)}) copy-start(f32[8192]{0:T(1024)} %param.25) | copy-start | bytes 98308
  134.1 15.9 %collective-permute-start.2 = (bf16[16,128,128]{2,1,0:T(8,128)(2,1)S(1)}, bf16[16,128,128]{2,1,0:T(8,128)(2,1)S(1)}, u32[]{:S(2)}, u32[]{:S(2)}) collective-permute-start(bf16[16,128,128]{2,1,0:T(8,128)(2,1)S(1)} %bitcast.50), channel_id=1, source_target_pairs={{0,1},{1,2},{2,3},{3,0},{4,5},{5,6},{6,7},{7,4},{8,9},{9,10},{10,1... | collective-permute-start | bytes 1572872 | tf_op jit(solution)/shard_map/ppermute | solution.py:295
  136.6 17.9 %collective-permute-start.3 = (bf16[16,128,128]{2,1,0:T(8,128)(2,1)S(1)}, bf16[16,128,128]{2,1,0:T(8,128)(2,1)S(1)}, u32[]{:S(2)}, u32[]{:S(2)}) collective-permute-start(bf16[16,128,128]{2,1,0:T(8,128)(2,1)S(1)} %bitcast.51), channel_id=1, source_target_pairs={{0,2},{1,3},{2,0},{3,1},{4,6},{5,7},{6,4},{7,5},{8,10},{9,11},{10,... | collective-permute-start | bytes 1572872 | tf_op jit(solution)/shard_map/ppermute | solution.py:295
  139.9 21.2 %collective-permute-start.4 = (bf16[16,128,128]{2,1,0:T(8,128)(2,1)S(1)}, bf16[16,128,128]{2,1,0:T(8,128)(2,1)S(1)}, u32[]{:S(2)}, u32[]{:S(2)}) collective-permute-start(bf16[16,128,128]{2,1,0:T(8,128)(2,1)S(1)} %bitcast.52), channel_id=1, source_target_pairs={{0,3},{1,0},{2,1},{3,2},{4,7},{5,4},{6,5},{7,6},{8,11},{9,8},{10,9... | collective-permute-start | bytes 1572872 | tf_op jit(solution)/shard_map/ppermute | solution.py:295
  161.1 27.9 %copy-start.6 = (s32[1024]{0:T(1024)S(1)}, s32[1024]{0:T(1024)}, u32[]{:S(2)}) copy-start(s32[1024]{0:T(1024)} %param.29) | copy-start | bytes 12292
Sparse Core Ops, SparseCore 0:
  33.5 100.1 all-gather.6

commit v3 on v2

--- a/solution.py
+++ b/solution.py
@@ -161,11 +161,12 @@
                 block = jnp.concatenate([weight[j, k, half] for k in range(NX)], axis=1)
                 result = result + dot(normed, block)
     for k in range(NX):
-        out[k] = result[:, k * ROWS : (k + 1) * ROWS]
+        out[k] = result[:, k * ROWS : (k + 1) * ROWS].astype(BF16)
 
 
 def residual_kernel(parts, residual, mixer_out, summed):
-    mixed = ((parts[0] + parts[1]) + (parts[2] + parts[3])).astype(BF16)
+    terms = [parts[k].astype(F32) for k in range(NX)]
+    mixed = ((terms[0] + terms[1]) + (terms[2] + terms[3])).astype(BF16)
     mixer_out[...] = mixed
     summed[...] = (residual[...].astype(F32) + mixed.astype(F32)).astype(BF16)
 
@@ -363,7 +364,7 @@
     )(mine)
     squares = lax.all_to_all(squares, ("zl", "x"), 0, 0)
     parts = call(
-        project_kernel, jax.ShapeDtypeStruct((NX, ROWS, ROWS), F32), [smem()] + [vmem()] * 6
+        project_kernel, jax.ShapeDtypeStruct((NX, ROWS, ROWS), BF16), [smem()] + [vmem()] * 6
     )(place, mine, paired, squares, mixer_gain.reshape(-1, CHANNELS), same, other)
     parts = lax.all_to_all(parts, "x", 0, 0)
     half = jax.ShapeDtypeStruct((ROWS, ROWS), BF16)

time: 211 us -> 211 us (level)
  no operation moved by 1% of the time
where the time goes in v3:
time: 211 us; the launch traced here: 210 us
  blocking collectives  123 us (58%)
  starting transfers between devices  30.1 us (14%)
  waiting for transfers between devices  19.2 us (9%)
  Pallas kernels  17.8 us (8%)
  between operations  14.3 us (7%)
  local copies, waits for them, and re-layouts  5.3 us (3%)
    all_gather x1, blocking collectives, local(): mine = lax.all_gather(gated, 'zg')  31.2 us
    all_gather x1, blocking collectives, local(): column = lax.all_gather(summed, ('zg', 'zl'))  26.3 us
    all_to_all x1, blocking collectives, local(): stats = lax.all_to_all(stats, MP, 0, 0, tiled=True)  25.1 us
    ppermute x4, starting transfers between devices, shifted(): return lax.ppermute(part, axis, [(i, (i + k) % n) for i in range(n)])  18.4 us
    all_to_all x1, blocking collectives, local(): sums = lax.all_to_all(sums, SEQ, 0, 0, tiled=True)  12.9 us
    ppermute x4, waiting for transfers between devices, shifted(): return lax.ppermute(part, axis, [(i, (i + k) % n) for i in range(n)])  11.2 us
    all_gather x1, blocking collectives, local(): chips = lax.all_gather(chip, 'y')  9.96 us
    all_to_all x1, blocking collectives, local(): parts = lax.all_to_all(parts, 'x', 0, 0)  8.99 us
  transfers between devices with their start and end apart: 8, of which 4 were waited for; matrix products, arithmetic and copies ran while one was open for 0% of the time, Pallas kernels for 5%

profile of v3, /device:TPU:1, one launch (start us, length us, event | category | flops | bytes accessed | tf_op | source)
XLA Modules:
  0.0 210.0 jit_solution(2945703792316373153)
XLA Ops:
  7.2 1.5 constant_dynamic-slice_fusion
  8.8 1.1 copy.24
  9.9 1.8 broadcast_in_dim.8
  11.9 1.8 shard_map.166
  13.7 8.7 %all-gather = f32[528,256]{1,0:T(8,128)S(1)} all-gather(f32[264,256]{1,0:T(8,128)S(1)} %get-tuple-element.22), channel_id=2, replica_groups=mesh['y'=4,'core'=2,'zg'=8,'zl'=2,'x'=4] {'core'}, dimensions={0}, use_global_device_ids=true | all-gather | bytes 811008 | tf_op jit(solution)/shard_map/all_gather | solution.py:347
  22.4 10.0 %all-gather.1 = bf16[1088,256]{1,0:T(8,128)(2,1)S(1)} all-gather(bf16[272,256]{1,0:T(8,128)(2,1)S(1)} %shard_map.167), channel_id=3, replica_groups=mesh['y'=4,'core'=2,'zg'=8,'zl'=2,'x'=4] {'y'}, dimensions={0}, use_global_device_ids=true | all-gather | bytes 696320 | tf_op jit(solution)/shard_map/all_gather | solution.py:349
  32.4 0.9 shard_map.168
  33.3 3.9 %all-to-all-start = ((bf16[16,2,256,128]{3,2,1,0:T(8,128)(2,1)}), bf16[16,2,256,128]{3,2,1,0:T(8,128)(2,1)S(1)}, u32[]{:S(2)}, u32[]{:S(2)}) async-start(bf16[16,2,256,128]{3,2,1,0:T(8,128)(2,1)} %bitcast.72), calls=%async_computation | async-start | bytes 4194304 | tf_op jit(solution)/shard_map/all_to_all | solution.py:354
  37.2 31.2 %all-gather.2 = bf16[1024,256]{1,0:T(8,128)(2,1)S(1)} all-gather(bf16[128,256]{1,0:T(8,128)(2,1)S(1)} %shard_map.168), channel_id=4, replica_groups=mesh['y'=4,'core'=2,'zg'=8,'zl'=2,'x'=4] {'zg'}, dimensions={0}, use_global_device_ids=true | all-gather | bytes 589824 | tf_op jit(solution)/shard_map/all_gather | solution.py:356
  68.4 9.7 %collective-permute-start.1 = (bf16[4,4,2,256,128]{4,3,2,1,0:T(8,128)(2,1)S(1)}, bf16[4,4,2,256,128]{4,3,2,1,0:T(8,128)(2,1)}, u32[]{:S(2)}, u32[]{:S(2)}) collective-permute-start(bf16[4,4,2,256,128]{4,3,2,1,0:T(8,128)(2,1)S(1)} %bitcast.42), channel_id=1, source_target_pairs={{0,64},{64,0},{1,65},{65,1},{2,66},{66,2},{3,67},{67,3},{4,68},{68... | collective-permute-start | bytes 6291464 | tf_op jit(solution)/shard_map/ppermute | solution.py:296
  78.1 3.5 %collective-permute-start = (bf16[8,128,256]{2,1,0:T(8,128)(2,1)S(1)}, bf16[8,128,256]{2,1,0:T(8,128)(2,1)S(1)}, u32[]{:S(2)}, u32[]{:S(2)}) collective-permute-start(bf16[8,128,256]{2,1,0:T(8,128)(2,1)S(1)} %bitcast.46), channel_id=1, source_target_pairs={{4,8},{12,16},{20,24},{28,32},{36,40},{44,48},{52,56},{60,0},{8,4}... | collective-permute-start | bytes 1572872 | tf_op jit(solution)/shard_map/ppermute | solution.py:361
  81.7 0.9 shard_map.169
  82.5 4.3 %all-to-all-start.1 = ((f32[8,8,128]{2,1,0:T(8,128)}), f32[8,8,128]{2,1,0:T(8,128)S(1)}, u32[]{:S(2)}, u32[]{:S(2)}) async-start(f32[8,8,128]{2,1,0:T(8,128)} %shard_map.169), calls=%async_computation.1 | async-start | bytes 65536 | tf_op jit(solution)/shard_map/all_to_all | solution.py:365
  86.9 5.1 %all-to-all-done.1.squares = f32[8,8,128]{2,1,0:T(8,128)S(1)} async-done(((f32[8,8,128]{2,1,0:T(8,128)}), f32[8,8,128]{2,1,0:T(8,128)S(1)}, u32[]{:S(2)}, u32[]{:S(2)}) %all-to-all-start.1) | async-done | bytes 32800 | tf_op jit(solution)/shard_map/all_to_all | solution.py:365
  91.9 3.0 %collective-permute-done.paired = bf16[8,128,256]{2,1,0:T(8,128)(2,1)S(1)} collective-permute-done((bf16[8,128,256]{2,1,0:T(8,128)(2,1)S(1)}, bf16[8,128,256]{2,1,0:T(8,128)(2,1)S(1)}, u32[]{:S(2)}, u32[]{:S(2)}) %collective-permute-start) | collective-permute-done | bytes 524320 | tf_op jit(solution)/shard_map/ppermute | solution.py:361
  94.9 2.5 %shard_map.170 = bf16[4,128,128]{2,1,0:T(8,128)(2,1)S(1)} custom-call(s32[7]{0:T(128)S(1)} %stack.31.place, bf16[8,128,256]{2,1,0:T(8,128)(2,1)S(1)} %bitcast.48, bf16[8,128,256]{2,1,0:T(8,128)(2,1)S(1)} %collective-permute-done.paired, f32[8,8,128]{2,1,0:T(8,128)S(1)} %all-to-all-done.1.squares, f32[64,256]{1,0:T(8,128)S(1)} %reshape.52.gain, ...), custom_call_target="tpu_custom_call" | custom-call | tf_op jit(solution)/shard_map/pallas_call | solution.py:366
  97.4 9.0 %all_to_all.37.parts = bf16[4,128,128]{2,1,0:T(8,128)(2,1)S(1)} all-to-all(bf16[4,128,128]{2,1,0:T(8,128)(2,1)S(1)} %shard_map.170), channel_id=1, replica_groups=mesh['y'=4,'core'=2,'zg'=8,'zl'=2,'x'=4] {'x'}, dimensions={0} | all-to-all | bytes 262144 | tf_op jit(solution)/shard_map/all_to_all | solution.py:369
  106.4 0.6 shard_map.171
  107.0 26.3 %all-gather.3 = bf16[2048,128]{1,0:T(8,128)(2,1)S(1)} all-gather(bf16[128,128]{1,0:T(8,128)(2,1)S(1)} %get-tuple-element.30), channel_id=5, replica_groups=mesh['y'=4,'core'=2,'zg'=8,'zl'=2,'x'=4] {'zg','zl'}, dimensions={0}, use_global_device_ids=true | all-gather | bytes 557056 | tf_op jit(solution)/shard_map/all_gather | solution.py:373
  133.4 2.5 %collective-permute-start.2 = (bf16[16,128,128]{2,1,0:T(8,128)(2,1)S(1)}, bf16[16,128,128]{2,1,0:T(8,128)(2,1)S(1)}, u32[]{:S(2)}, u32[]{:S(2)}) collective-permute-start(bf16[16,128,128]{2,1,0:T(8,128)(2,1)S(1)} %bitcast.50), channel_id=1, source_target_pairs={{0,1},{1,2},{2,3},{3,0},{4,5},{5,6},{6,7},{7,4},{8,9},{9,10},{10,1... | collective-permute-start | bytes 1572872 | tf_op jit(solution)/shard_map/ppermute | solution.py:296
  135.9 3.3 %collective-permute-start.3 = (bf16[16,128,128]{2,1,0:T(8,128)(2,1)S(1)}, bf16[16,128,128]{2,1,0:T(8,128)(2,1)S(1)}, u32[]{:S(2)}, u32[]{:S(2)}) collective-permute-start(bf16[16,128,128]{2,1,0:T(8,128)(2,1)S(1)} %bitcast.51), channel_id=1, source_target_pairs={{0,2},{1,3},{2,0},{3,1},{4,6},{5,7},{6,4},{7,5},{8,10},{9,11},{10,... | collective-permute-start | bytes 1572872 | tf_op jit(solution)/shard_map/ppermute | solution.py:296
  139.3 2.9 %collective-permute-start.4 = (bf16[16,128,128]{2,1,0:T(8,128)(2,1)S(1)}, bf16[16,128,128]{2,1,0:T(8,128)(2,1)S(1)}, u32[]{:S(2)}, u32[]{:S(2)}) collective-permute-start(bf16[16,128,128]{2,1,0:T(8,128)(2,1)S(1)} %bitcast.52), channel_id=1, source_target_pairs={{0,3},{1,0},{2,1},{3,2},{4,7},{5,4},{6,5},{7,6},{8,11},{9,8},{10,9... | collective-permute-start | bytes 1572872 | tf_op jit(solution)/shard_map/ppermute | solution.py:296
  142.2 0.1 copy.27.wanted
  142.4 6.9 %shard_map.172 = (f32[128,1024]{1,0:T(8,128)S(1)}, f32[128,128]{1,0:T(8,128)S(1)}, bf16[8,3,2,128,1024]{4,3,2,1,0:T(8,128)(2,1)S(1)}) custom-call(s32[7]{0:T(128)S(1)} %stack.31.place, bf16[16,128,128]{2,1,0:T(8,128)(2,1)S(1)} %bitcast.53, f32[16,4,1,128]{3,2,1,0:T(1,128)S(1)} %bitcast.59, bf16[8,2,4,128,1024]{4,3,2,1,0:T(8,128)(2,1)} %bitcast.71), custom_call_target="tpu_custom_call" | custom-call | flops 536870912 | bytes 16777216 | tf_op jit(solution)/shard_map/pallas_call | solution.py:237
  149.3 4.5 %collective-permute-done.3.p2 = bf16[16,128,128]{2,1,0:T(8,128)(2,1)S(1)} collective-permute-done((bf16[16,128,128]{2,1,0:T(8,128)(2,1)S(1)}, bf16[16,128,128]{2,1,0:T(8,128)(2,1)S(1)}, u32[]{:S(2)}, u32[]{:S(2)}) %collective-permute-start.3) | collective-permute-done | bytes 524320 | tf_op jit(solution)/shard_map/ppermute | solution.py:296
  153.8 6.7 %collective-permute-done.4.p3 = bf16[16,128,128]{2,1,0:T(8,128)(2,1)S(1)} collective-permute-done((bf16[16,128,128]{2,1,0:T(8,128)(2,1)S(1)}, bf16[16,128,128]{2,1,0:T(8,128)(2,1)S(1)}, u32[]{:S(2)}, u32[]{:S(2)}) %collective-permute-start.4) | collective-permute-done | bytes 524320 | tf_op jit(solution)/shard_map/ppermute | solution.py:296
  160.4 2.8 %shard_map.173 = f32[128,128]{1,0:T(8,128)S(1)} custom-call(s32[7]{0:T(128)S(1)} %stack.31.place, bf16[16,128,128]{2,1,0:T(8,128)(2,1)S(1)} %collective-permute-done.2.p1, bf16[16,128,128]{2,1,0:T(8,128)(2,1)S(1)} %collective-permute-done.3.p2, bf16[16,128,128]{2,1,0:T(8,128)(2,1)S(1)} %collective-permute-done.4.p3, f32[16,4,1,128]{3,2,1,0:T(1,128)S(1)} %bitcast.60, ...), custom_call_target="tpu_custom_call" | custom-call | flops 536870912 | bytes 16777216 | tf_op jit(solution)/shard_map/pallas_call | solution.py:253
  163.2 25.1 %all_to_all.38 = f32[64,2,128]{2,1,0:T(2,128)S(1)} all-to-all(f32[64,2,128]{2,1,0:T(2,128)S(1)} %bitcast.56), channel_id=1, replica_groups=mesh['y'=4,'core'=2,'zg'=8,'zl'=2,'x'=4] {'zg','zl','x'}, dimensions={0} | all-to-all | bytes 131072 | tf_op jit(solution)/shard_map/all_to_all | solution.py:379
  188.3 1.1 shard_map.174
  189.5 12.9 %all_to_all.39 = f32[8,1,128]{2,1,0:T(1,128)S(1)} all-to-all(f32[8,1,128]{2,1,0:T(1,128)S(1)} %bitcast.67), channel_id=1, replica_groups=mesh['y'=4,'core'=2,'zg'=8,'zl'=2,'x'=4] {'y','core'}, dimensions={0} | all-to-all | bytes 8192 | tf_op jit(solution)/shard_map/all_to_all | solution.py:385
  202.3 0.3 shard_map.175
  202.6 0.5 slice_bitcast_fusion
  (34 shorter events, 0.4 us)
Async XLA Ops:
  7.2 135.0 %copy-start = (s32[1024]{0:T(1024)S(1)}, s32[1024]{0:T(1024)}, u32[]{:S(2)}) copy-start(s32[1024]{0:T(1024)} %param.27) | copy-start | bytes 12292
  7.2 135.2 %all-gather.7.cloned.1.call-start = ((), (), s32[]{:S(2)}) async-start(), calls=%async_computation.5 | async-start | bytes 18874368 | tf_op jit(solution)/shard_map/all_gather | solution.py:355
  8.7 3.1 %copy-start.2 = (bf16[128,256]{1,0:T(8,128)(2,1)S(1)}, bf16[128,256]{1,0:T(8,128)(2,1)}, u32[]{:S(2)}) copy-start(bf16[128,256]{1,0:T(8,128)(2,1)} %x_ref.1) | copy-start | bytes 196612
  8.7 3.1 %copy-start.4 = (s32[1024]{0:T(1024)S(1)}, s32[1024]{0:T(1024)}, u32[]{:S(2)}) copy-start(s32[1024]{0:T(1024)} %param.28) | copy-start | bytes 12292
  8.7 3.1 %copy-start.7 = (f32[128,4]{0,1:T(4,128)S(1)}, f32[128,4]{0,1:T(4,128)}, u32[]{:S(2)}) copy-start(f32[128,4]{0,1:T(4,128)} %param.20) | copy-start | bytes 6148
  8.8 3.1 %copy-start.8 = (f32[4]{0:T(128)S(1)}, f32[4]{0:T(128)}, u32[]{:S(2)}) copy-start(f32[4]{0:T(128)} %param.21) | copy-start | bytes 52
  8.8 3.1 %copy-start.9 = (f32[4]{0:T(128)S(1)}, f32[4]{0:T(128)}, u32[]{:S(2)}) copy-start(f32[4]{0:T(128)} %param.22) | copy-start | bytes 52
  9.9 22.5 %copy-start.3 = (bf16[128,256]{1,0:T(8,128)(2,1)S(1)}, bf16[128,256]{1,0:T(8,128)(2,1)}, u32[]{:S(2)}) copy-start(bf16[128,256]{1,0:T(8,128)(2,1)} %gate.1) | copy-start | bytes 196612
  33.3 53.5 %copy-start.10 = (f32[16384]{0:T(1024)S(1)}, f32[16384]{0:T(1024)}, u32[]{:S(2)}) copy-start(f32[16384]{0:T(1024)} %param.23) | copy-start | bytes 196612
  33.3 35.1 %all-to-all-start = ((bf16[16,2,256,128]{3,2,1,0:T(8,128)(2,1)}), bf16[16,2,256,128]{3,2,1,0:T(8,128)(2,1)S(1)}, u32[]{:S(2)}, u32[]{:S(2)}) async-start(bf16[16,2,256,128]{3,2,1,0:T(8,128)(2,1)} %bitcast.72), calls=%async_computation | async-start | bytes 4194304 | tf_op jit(solution)/shard_map/all_to_all | solution.py:354
  68.4 26.4 %collective-permute-start.1 = (bf16[4,4,2,256,128]{4,3,2,1,0:T(8,128)(2,1)S(1)}, bf16[4,4,2,256,128]{4,3,2,1,0:T(8,128)(2,1)}, u32[]{:S(2)}, u32[]{:S(2)}) collective-permute-start(bf16[4,4,2,256,128]{4,3,2,1,0:T(8,128)(2,1)S(1)} %bitcast.42), channel_id=1, source_target_pairs={{0,64},{64,0},{1,65},{65,1},{2,66},{66,2},{3,67},{67,3},{4,68},{68... | collective-permute-start | bytes 6291464 | tf_op jit(solution)/shard_map/ppermute | solution.py:296
  78.1 16.8 %collective-permute-start = (bf16[8,128,256]{2,1,0:T(8,128)(2,1)S(1)}, bf16[8,128,256]{2,1,0:T(8,128)(2,1)S(1)}, u32[]{:S(2)}, u32[]{:S(2)}) collective-permute-start(bf16[8,128,256]{2,1,0:T(8,128)(2,1)S(1)} %bitcast.46), channel_id=1, source_target_pairs={{4,8},{12,16},{20,24},{28,32},{36,40},{44,48},{52,56},{60,0},{8,4}... | collective-permute-start | bytes 1572872 | tf_op jit(solution)/shard_map/ppermute | solution.py:361
  82.5 9.4 %all-to-all-start.1 = ((f32[8,8,128]{2,1,0:T(8,128)}), f32[8,8,128]{2,1,0:T(8,128)S(1)}, u32[]{:S(2)}, u32[]{:S(2)}) async-start(f32[8,8,128]{2,1,0:T(8,128)} %shard_map.169), calls=%async_computation.1 | async-start | bytes 65536 | tf_op jit(solution)/shard_map/all_to_all | solution.py:365
  86.8 19.6 %copy-start.5 = (bf16[128,128]{1,0:T(8,128)(2,1)S(1)}, bf16[128,128]{1,0:T(8,128)(2,1)}, u32[]{:S(2)}) copy-start(bf16[128,128]{1,0:T(8,128)(2,1)} %residual.1) | copy-start | bytes 98308
  86.8 55.5 %copy-start.1 = (f32[8192]{0:T(1024)S(1)}, f32[8192]{0:T(1024)}, u32[]{:S(2)}) copy-start(f32[8192]{0:T(1024)} %param.25) | copy-start | bytes 98308
  133.4 15.9 %collective-permute-start.2 = (bf16[16,128,128]{2,1,0:T(8,128)(2,1)S(1)}, bf16[16,128,128]{2,1,0:T(8,128)(2,1)S(1)}, u32[]{:S(2)}, u32[]{:S(2)}) collective-permute-start(bf16[16,128,128]{2,1,0:T(8,128)(2,1)S(1)} %bitcast.50), channel_id=1, source_target_pairs={{0,1},{1,2},{2,3},{3,0},{4,5},{5,6},{6,7},{7,4},{8,9},{9,10},{10,1... | collective-permute-start | bytes 1572872 | tf_op jit(solution)/shard_map/ppermute | solution.py:296
  135.9 17.9 %collective-permute-start.3 = (bf16[16,128,128]{2,1,0:T(8,128)(2,1)S(1)}, bf16[16,128,128]{2,1,0:T(8,128)(2,1)S(1)}, u32[]{:S(2)}, u32[]{:S(2)}) collective-permute-start(bf16[16,128,128]{2,1,0:T(8,128)(2,1)S(1)} %bitcast.51), channel_id=1, source_target_pairs={{0,2},{1,3},{2,0},{3,1},{4,6},{5,7},{6,4},{7,5},{8,10},{9,11},{10,... | collective-permute-start | bytes 1572872 | tf_op jit(solution)/shard_map/ppermute | solution.py:296
  139.3 21.2 %collective-permute-start.4 = (bf16[16,128,128]{2,1,0:T(8,128)(2,1)S(1)}, bf16[16,128,128]{2,1,0:T(8,128)(2,1)S(1)}, u32[]{:S(2)}, u32[]{:S(2)}) collective-permute-start(bf16[16,128,128]{2,1,0:T(8,128)(2,1)S(1)} %bitcast.52), channel_id=1, source_target_pairs={{0,3},{1,0},{2,1},{3,2},{4,7},{5,4},{6,5},{7,6},{8,11},{9,8},{10,9... | collective-permute-start | bytes 1572872 | tf_op jit(solution)/shard_map/ppermute | solution.py:296
  160.4 27.9 %copy-start.6 = (s32[1024]{0:T(1024)S(1)}, s32[1024]{0:T(1024)}, u32[]{:S(2)}) copy-start(s32[1024]{0:T(1024)} %param.29) | copy-start | bytes 12292
Sparse Core Ops, SparseCore 0:
  33.5 100.1 all-gather.6

commit v4 on v2

--- a/solution.py
+++ b/solution.py
@@ -22,6 +22,7 @@
 STATE = 256
 GROUPS = 8
 MSG = STATE + 16
+ORDER = (0, 2, 1, 3)
 
 
 def dot(a, b, precision=None):
@@ -183,7 +184,7 @@
 def own_kernel(place, part, gain, weight, total, squares, later, held, arrived):
     copies = []
     for k in range(NX):
-        source = lax.rem(place[4] + NX - k, NX)
+        source = lax.rem(place[4] + NX - ORDER[k], NX)
         for g in range(NG):
             for half in range(NL):
                 target = later.at[g, k - 1, half] if k else held.at[g, half]
@@ -208,7 +209,7 @@
 
 def rest_kernel(place, p1, p2, p3, gain, weight, total, squares, wanted, out):
     parts = (p1, p2, p3)
-    sources = [lax.rem(place[4] + NX - k, NX) for k in range(1, NX)]
+    sources = [lax.rem(place[4] + NX - k, NX) for k in ORDER[1:]]
     result = total[...]
     square = squares[...]
     for g in range(NG):
@@ -370,7 +371,7 @@
     mixer_out, summed = call(residual_kernel, (half, half), [vmem()] * 2)(parts, residual_in)
 
     column = lax.all_gather(summed, ("zg", "zl"))
-    features = [column] + [shifted(column, "x", k) for k in range(1, NX)]
+    features = [column] + [shifted(column, "x", k) for k in ORDER[1:]]
     wanted = lax.dynamic_slice_in_dim(targets, seq * ROWS, ROWS).reshape(ROWS, 1)
     gains = final_gain.reshape(NZ, NX, 1, ROWS)
     matrix = head_rows.reshape(NG, NL, NX, ROWS, -1)

time: 211 us -> 208 us (0.986)
    all_to_all x1, blocking collectives: 25.1 us -> 22.6 us  [local(): stats = lax.all_to_all(stats, MP, 0, 0, tiled=True)]
  transfers between devices with their start and end apart: 8 -> 8, of which waited for: 4 -> 3; matrix products, arithmetic and copies ran while one was open for 0% -> 0% of each run, Pallas kernels for 5% -> 5%
where the time goes in v4:
time: 208 us; the launch traced here: 207 us
  blocking collectives  122 us (59%)
  starting transfers between devices  30.7 us (15%)
  Pallas kernels  17.8 us (9%)
  waiting for transfers between devices  17.5 us (8%)
  between operations  14.3 us (7%)
  local copies, waits for them, and re-layouts  5.3 us (3%)
    all_gather x1, blocking collectives, local(): mine = lax.all_gather(gated, 'zg')  31.2 us
    all_gather x1, blocking collectives, local(): column = lax.all_gather(summed, ('zg', 'zl'))  26.3 us
    all_to_all x1, blocking collectives, local(): stats = lax.all_to_all(stats, MP, 0, 0, tiled=True)  22.6 us
    ppermute x4, starting transfers between devices, shifted(): return lax.ppermute(part, axis, [(i, (i + k) % n) for i in range(n)])  19 us
    all_to_all x1, blocking collectives, local(): sums = lax.all_to_all(sums, SEQ, 0, 0, tiled=True)  13.4 us
    all_gather x1, blocking collectives, local(): chips = lax.all_gather(chip, 'y')  9.96 us
    all_to_all x1, blocking collectives, local(): parts = lax.all_to_all(parts, 'x', 0, 0)  9.69 us
    ppermute x4, waiting for transfers between devices, shifted(): return lax.ppermute(part, axis, [(i, (i + k) % n) for i in range(n)])  9.46 us
  transfers between devices with their start and end apart: 8, of which 3 were waited for; matrix products, arithmetic and copies ran while one was open for 0% of the time, Pallas kernels for 5%

profile of v4, /device:TPU:1, one launch (start us, length us, event | category | flops | bytes accessed | tf_op | source)
XLA Modules:
  0.0 207.4 jit_solution(12472436125761566440)
XLA Ops:
  7.2 1.5 constant_dynamic-slice_fusion
  8.8 1.1 copy.24
  9.9 1.8 broadcast_in_dim.8
  11.7 0.1 stack.31.place
  11.9 1.8 shard_map.166
  13.7 8.7 %all-gather = f32[528,256]{1,0:T(8,128)S(1)} all-gather(f32[264,256]{1,0:T(8,128)S(1)} %get-tuple-element.22), channel_id=2, replica_groups=mesh['y'=4,'core'=2,'zg'=8,'zl'=2,'x'=4] {'core'}, dimensions={0}, use_global_device_ids=true | all-gather | bytes 811008 | tf_op jit(solution)/shard_map/all_gather | solution.py:347
  22.4 10.0 %all-gather.1 = bf16[1088,256]{1,0:T(8,128)(2,1)S(1)} all-gather(bf16[272,256]{1,0:T(8,128)(2,1)S(1)} %shard_map.167), channel_id=3, replica_groups=mesh['y'=4,'core'=2,'zg'=8,'zl'=2,'x'=4] {'y'}, dimensions={0}, use_global_device_ids=true | all-gather | bytes 696320 | tf_op jit(solution)/shard_map/all_gather | solution.py:349
  32.4 0.9 shard_map.168
  33.3 3.9 %all-to-all-start = ((bf16[16,2,256,128]{3,2,1,0:T(8,128)(2,1)}), bf16[16,2,256,128]{3,2,1,0:T(8,128)(2,1)S(1)}, u32[]{:S(2)}, u32[]{:S(2)}) async-start(bf16[16,2,256,128]{3,2,1,0:T(8,128)(2,1)} %bitcast.72), calls=%async_computation | async-start | bytes 4194304 | tf_op jit(solution)/shard_map/all_to_all | solution.py:354
  37.2 31.2 %all-gather.2 = bf16[1024,256]{1,0:T(8,128)(2,1)S(1)} all-gather(bf16[128,256]{1,0:T(8,128)(2,1)S(1)} %shard_map.168), channel_id=4, replica_groups=mesh['y'=4,'core'=2,'zg'=8,'zl'=2,'x'=4] {'zg'}, dimensions={0}, use_global_device_ids=true | all-gather | bytes 589824 | tf_op jit(solution)/shard_map/all_gather | solution.py:356
  68.4 9.7 %collective-permute-start.1 = (bf16[4,4,2,256,128]{4,3,2,1,0:T(8,128)(2,1)S(1)}, bf16[4,4,2,256,128]{4,3,2,1,0:T(8,128)(2,1)}, u32[]{:S(2)}, u32[]{:S(2)}) collective-permute-start(bf16[4,4,2,256,128]{4,3,2,1,0:T(8,128)(2,1)S(1)} %bitcast.42), channel_id=1, source_target_pairs={{0,64},{64,0},{1,65},{65,1},{2,66},{66,2},{3,67},{67,3},{4,68},{68... | collective-permute-start | bytes 6291464 | tf_op jit(solution)/shard_map/ppermute | solution.py:296
  78.1 3.5 %collective-permute-start = (bf16[8,128,256]{2,1,0:T(8,128)(2,1)S(1)}, bf16[8,128,256]{2,1,0:T(8,128)(2,1)S(1)}, u32[]{:S(2)}, u32[]{:S(2)}) collective-permute-start(bf16[8,128,256]{2,1,0:T(8,128)(2,1)S(1)} %bitcast.46), channel_id=1, source_target_pairs={{4,8},{12,16},{20,24},{28,32},{36,40},{44,48},{52,56},{60,0},{8,4}... | collective-permute-start | bytes 1572872 | tf_op jit(solution)/shard_map/ppermute | solution.py:361
  81.7 0.9 shard_map.169
  82.5 4.3 %all-to-all-start.1 = ((f32[8,8,128]{2,1,0:T(8,128)}), f32[8,8,128]{2,1,0:T(8,128)S(1)}, u32[]{:S(2)}, u32[]{:S(2)}) async-start(f32[8,8,128]{2,1,0:T(8,128)} %shard_map.169), calls=%async_computation.1 | async-start | bytes 65536 | tf_op jit(solution)/shard_map/all_to_all | solution.py:365
  86.9 5.1 %all-to-all-done.1.squares = f32[8,8,128]{2,1,0:T(8,128)S(1)} async-done(((f32[8,8,128]{2,1,0:T(8,128)}), f32[8,8,128]{2,1,0:T(8,128)S(1)}, u32[]{:S(2)}, u32[]{:S(2)}) %all-to-all-start.1) | async-done | bytes 32800 | tf_op jit(solution)/shard_map/all_to_all | solution.py:365
  91.9 3.0 %collective-permute-done.paired = bf16[8,128,256]{2,1,0:T(8,128)(2,1)S(1)} collective-permute-done((bf16[8,128,256]{2,1,0:T(8,128)(2,1)S(1)}, bf16[8,128,256]{2,1,0:T(8,128)(2,1)S(1)}, u32[]{:S(2)}, u32[]{:S(2)}) %collective-permute-start) | collective-permute-done | bytes 524320 | tf_op jit(solution)/shard_map/ppermute | solution.py:361
  94.9 2.5 %shard_map.170 = f32[4,128,128]{2,1,0:T(8,128)S(1)} custom-call(s32[7]{0:T(128)S(1)} %stack.31.place, bf16[8,128,256]{2,1,0:T(8,128)(2,1)S(1)} %bitcast.48, bf16[8,128,256]{2,1,0:T(8,128)(2,1)S(1)} %collective-permute-done.paired, f32[8,8,128]{2,1,0:T(8,128)S(1)} %all-to-all-done.1.squares, f32[64,256]{1,0:T(8,128)S(1)} %reshape.52.gain, ...), custom_call_target="tpu_custom_call" | custom-call | tf_op jit(solution)/shard_map/pallas_call | solution.py:366
  97.4 9.7 %all_to_all.37.parts = f32[4,128,128]{2,1,0:T(8,128)S(1)} all-to-all(f32[4,128,128]{2,1,0:T(8,128)S(1)} %shard_map.170), channel_id=1, replica_groups=mesh['y'=4,'core'=2,'zg'=8,'zl'=2,'x'=4] {'x'}, dimensions={0} | all-to-all | bytes 524288 | tf_op jit(solution)/shard_map/all_to_all | solution.py:369
  107.1 0.6 shard_map.171
  107.7 26.3 %all-gather.3 = bf16[2048,128]{1,0:T(8,128)(2,1)S(1)} all-gather(bf16[128,128]{1,0:T(8,128)(2,1)S(1)} %get-tuple-element.30), channel_id=5, replica_groups=mesh['y'=4,'core'=2,'zg'=8,'zl'=2,'x'=4] {'zg','zl'}, dimensions={0}, use_global_device_ids=true | all-gather | bytes 557056 | tf_op jit(solution)/shard_map/all_gather | solution.py:373
  134.1 2.8 %collective-permute-start.2 = (bf16[16,128,128]{2,1,0:T(8,128)(2,1)S(1)}, bf16[16,128,128]{2,1,0:T(8,128)(2,1)S(1)}, u32[]{:S(2)}, u32[]{:S(2)}) collective-permute-start(bf16[16,128,128]{2,1,0:T(8,128)(2,1)S(1)} %bitcast.50), channel_id=1, source_target_pairs={{0,2},{1,3},{2,0},{3,1},{4,6},{5,7},{6,4},{7,5},{8,10},{9,11},{10,... | collective-permute-start | bytes 1572872 | tf_op jit(solution)/shard_map/ppermute | solution.py:296
  136.9 2.5 %collective-permute-start.3 = (bf16[16,128,128]{2,1,0:T(8,128)(2,1)S(1)}, bf16[16,128,128]{2,1,0:T(8,128)(2,1)S(1)}, u32[]{:S(2)}, u32[]{:S(2)}) collective-permute-start(bf16[16,128,128]{2,1,0:T(8,128)(2,1)S(1)} %bitcast.51), channel_id=1, source_target_pairs={{0,1},{1,2},{2,3},{3,0},{4,5},{5,6},{6,7},{7,4},{8,9},{9,10},{10,1... | collective-permute-start | bytes 1572872 | tf_op jit(solution)/shard_map/ppermute | solution.py:296
  139.3 4.0 %collective-permute-start.4 = (bf16[16,128,128]{2,1,0:T(8,128)(2,1)S(1)}, bf16[16,128,128]{2,1,0:T(8,128)(2,1)S(1)}, u32[]{:S(2)}, u32[]{:S(2)}) collective-permute-start(bf16[16,128,128]{2,1,0:T(8,128)(2,1)S(1)} %bitcast.52), channel_id=1, source_target_pairs={{0,3},{1,0},{2,1},{3,2},{4,7},{5,4},{6,5},{7,6},{8,11},{9,8},{10,9... | collective-permute-start | bytes 1572872 | tf_op jit(solution)/shard_map/ppermute | solution.py:296
  143.5 0.1 copy.27.wanted
  143.6 6.9 %shard_map.172 = (f32[128,1024]{1,0:T(8,128)S(1)}, f32[128,128]{1,0:T(8,128)S(1)}, bf16[8,3,2,128,1024]{4,3,2,1,0:T(8,128)(2,1)S(1)}) custom-call(s32[7]{0:T(128)S(1)} %stack.31.place, bf16[16,128,128]{2,1,0:T(8,128)(2,1)S(1)} %bitcast.53, f32[16,4,1,128]{3,2,1,0:T(1,128)S(1)} %bitcast.59, bf16[8,2,4,128,1024]{4,3,2,1,0:T(8,128)(2,1)} %bitcast.71), custom_call_target="tpu_custom_call" | custom-call | flops 536870912 | bytes 16777216 | tf_op jit(solution)/shard_map/pallas_call | solution.py:237
  150.5 9.5 %collective-permute-done.3.p2 = bf16[16,128,128]{2,1,0:T(8,128)(2,1)S(1)} collective-permute-done((bf16[16,128,128]{2,1,0:T(8,128)(2,1)S(1)}, bf16[16,128,128]{2,1,0:T(8,128)(2,1)S(1)}, u32[]{:S(2)}, u32[]{:S(2)}) %collective-permute-start.3) | collective-permute-done | bytes 524320 | tf_op jit(solution)/shard_map/ppermute | solution.py:296
  159.9 2.8 %shard_map.173 = f32[128,128]{1,0:T(8,128)S(1)} custom-call(s32[7]{0:T(128)S(1)} %stack.31.place, bf16[16,128,128]{2,1,0:T(8,128)(2,1)S(1)} %collective-permute-done.2.p1, bf16[16,128,128]{2,1,0:T(8,128)(2,1)S(1)} %collective-permute-done.3.p2, bf16[16,128,128]{2,1,0:T(8,128)(2,1)S(1)} %collective-permute-done.4.p3, f32[16,4,1,128]{3,2,1,0:T(1,128)S(1)} %bitcast.60, ...), custom_call_target="tpu_custom_call" | custom-call | flops 536870912 | bytes 16777216 | tf_op jit(solution)/shard_map/pallas_call | solution.py:253
  162.7 22.6 %all_to_all.38 = f32[64,2,128]{2,1,0:T(2,128)S(1)} all-to-all(f32[64,2,128]{2,1,0:T(2,128)S(1)} %bitcast.56), channel_id=1, replica_groups=mesh['y'=4,'core'=2,'zg'=8,'zl'=2,'x'=4] {'zg','zl','x'}, dimensions={0} | all-to-all | bytes 131072 | tf_op jit(solution)/shard_map/all_to_all | solution.py:379
  185.3 1.1 shard_map.174
  186.4 13.4 %all_to_all.39 = f32[8,1,128]{2,1,0:T(1,128)S(1)} all-to-all(f32[8,1,128]{2,1,0:T(1,128)S(1)} %bitcast.67), channel_id=1, replica_groups=mesh['y'=4,'core'=2,'zg'=8,'zl'=2,'x'=4] {'y','core'}, dimensions={0} | all-to-all | bytes 8192 | tf_op jit(solution)/shard_map/all_to_all | solution.py:385
  199.8 0.3 shard_map.175
  200.1 0.5 slice_bitcast_fusion
  (34 shorter events, 0.3 us)
Async XLA Ops:
  7.2 136.2 %copy-start = (s32[1024]{0:T(1024)S(1)}, s32[1024]{0:T(1024)}, u32[]{:S(2)}) copy-start(s32[1024]{0:T(1024)} %param.27) | copy-start | bytes 12292
  7.2 136.4 %all-gather.7.cloned.1.call-start = ((), (), s32[]{:S(2)}) async-start(), calls=%async_computation.5 | async-start | bytes 18874368 | tf_op jit(solution)/shard_map/all_gather | solution.py:355
  8.7 3.1 %copy-start.2 = (bf16[128,256]{1,0:T(8,128)(2,1)S(1)}, bf16[128,256]{1,0:T(8,128)(2,1)}, u32[]{:S(2)}) copy-start(bf16[128,256]{1,0:T(8,128)(2,1)} %x_ref.1) | copy-start | bytes 196612
  8.7 3.1 %copy-start.4 = (s32[1024]{0:T(1024)S(1)}, s32[1024]{0:T(1024)}, u32[]{:S(2)}) copy-start(s32[1024]{0:T(1024)} %param.28) | copy-start | bytes 12292
  8.7 3.1 %copy-start.7 = (f32[128,4]{0,1:T(4,128)S(1)}, f32[128,4]{0,1:T(4,128)}, u32[]{:S(2)}) copy-start(f32[128,4]{0,1:T(4,128)} %param.20) | copy-start | bytes 6148
  8.8 3.1 %copy-start.8 = (f32[4]{0:T(128)S(1)}, f32[4]{0:T(128)}, u32[]{:S(2)}) copy-start(f32[4]{0:T(128)} %param.21) | copy-start | bytes 52
  8.8 3.1 %copy-start.9 = (f32[4]{0:T(128)S(1)}, f32[4]{0:T(128)}, u32[]{:S(2)}) copy-start(f32[4]{0:T(128)} %param.22) | copy-start | bytes 52
  9.9 22.5 %copy-start.3 = (bf16[128,256]{1,0:T(8,128)(2,1)S(1)}, bf16[128,256]{1,0:T(8,128)(2,1)}, u32[]{:S(2)}) copy-start(bf16[128,256]{1,0:T(8,128)(2,1)} %gate.1) | copy-start | bytes 196612
  33.3 53.5 %copy-start.10 = (f32[16384]{0:T(1024)S(1)}, f32[16384]{0:T(1024)}, u32[]{:S(2)}) copy-start(f32[16384]{0:T(1024)} %param.23) | copy-start | bytes 196612
  33.3 35.1 %all-to-all-start = ((bf16[16,2,256,128]{3,2,1,0:T(8,128)(2,1)}), bf16[16,2,256,128]{3,2,1,0:T(8,128)(2,1)S(1)}, u32[]{:S(2)}, u32[]{:S(2)}) async-start(bf16[16,2,256,128]{3,2,1,0:T(8,128)(2,1)} %bitcast.72), calls=%async_computation | async-start | bytes 4194304 | tf_op jit(solution)/shard_map/all_to_all | solution.py:354
  68.4 26.4 %collective-permute-start.1 = (bf16[4,4,2,256,128]{4,3,2,1,0:T(8,128)(2,1)S(1)}, bf16[4,4,2,256,128]{4,3,2,1,0:T(8,128)(2,1)}, u32[]{:S(2)}, u32[]{:S(2)}) collective-permute-start(bf16[4,4,2,256,128]{4,3,2,1,0:T(8,128)(2,1)S(1)} %bitcast.42), channel_id=1, source_target_pairs={{0,64},{64,0},{1,65},{65,1},{2,66},{66,2},{3,67},{67,3},{4,68},{68... | collective-permute-start | bytes 6291464 | tf_op jit(solution)/shard_map/ppermute | solution.py:296
  78.1 16.8 %collective-permute-start = (bf16[8,128,256]{2,1,0:T(8,128)(2,1)S(1)}, bf16[8,128,256]{2,1,0:T(8,128)(2,1)S(1)}, u32[]{:S(2)}, u32[]{:S(2)}) collective-permute-start(bf16[8,128,256]{2,1,0:T(8,128)(2,1)S(1)} %bitcast.46), channel_id=1, source_target_pairs={{4,8},{12,16},{20,24},{28,32},{36,40},{44,48},{52,56},{60,0},{8,4}... | collective-permute-start | bytes 1572872 | tf_op jit(solution)/shard_map/ppermute | solution.py:361
  82.5 9.4 %all-to-all-start.1 = ((f32[8,8,128]{2,1,0:T(8,128)}), f32[8,8,128]{2,1,0:T(8,128)S(1)}, u32[]{:S(2)}, u32[]{:S(2)}) async-start(f32[8,8,128]{2,1,0:T(8,128)} %shard_map.169), calls=%async_computation.1 | async-start | bytes 65536 | tf_op jit(solution)/shard_map/all_to_all | solution.py:365
  86.8 20.3 %copy-start.5 = (bf16[128,128]{1,0:T(8,128)(2,1)S(1)}, bf16[128,128]{1,0:T(8,128)(2,1)}, u32[]{:S(2)}) copy-start(bf16[128,128]{1,0:T(8,128)(2,1)} %residual.1) | copy-start | bytes 98308
  86.8 56.8 %copy-start.1 = (f32[8192]{0:T(1024)S(1)}, f32[8192]{0:T(1024)}, u32[]{:S(2)}) copy-start(f32[8192]{0:T(1024)} %param.25) | copy-start | bytes 98308
  134.1 16.4 %collective-permute-start.2 = (bf16[16,128,128]{2,1,0:T(8,128)(2,1)S(1)}, bf16[16,128,128]{2,1,0:T(8,128)(2,1)S(1)}, u32[]{:S(2)}, u32[]{:S(2)}) collective-permute-start(bf16[16,128,128]{2,1,0:T(8,128)(2,1)S(1)} %bitcast.50), channel_id=1, source_target_pairs={{0,2},{1,3},{2,0},{3,1},{4,6},{5,7},{6,4},{7,5},{8,10},{9,11},{10,... | collective-permute-start | bytes 1572872 | tf_op jit(solution)/shard_map/ppermute | solution.py:296
  136.9 23.1 %collective-permute-start.3 = (bf16[16,128,128]{2,1,0:T(8,128)(2,1)S(1)}, bf16[16,128,128]{2,1,0:T(8,128)(2,1)S(1)}, u32[]{:S(2)}, u32[]{:S(2)}) collective-permute-start(bf16[16,128,128]{2,1,0:T(8,128)(2,1)S(1)} %bitcast.51), channel_id=1, source_target_pairs={{0,1},{1,2},{2,3},{3,0},{4,5},{5,6},{6,7},{7,4},{8,9},{9,10},{10,1... | collective-permute-start | bytes 1572872 | tf_op jit(solution)/shard_map/ppermute | solution.py:296
  139.3 20.6 %collective-permute-start.4 = (bf16[16,128,128]{2,1,0:T(8,128)(2,1)S(1)}, bf16[16,128,128]{2,1,0:T(8,128)(2,1)S(1)}, u32[]{:S(2)}, u32[]{:S(2)}) collective-permute-start(bf16[16,128,128]{2,1,0:T(8,128)(2,1)S(1)} %bitcast.52), channel_id=1, source_target_pairs={{0,3},{1,0},{2,1},{3,2},{4,7},{5,4},{6,5},{7,6},{8,11},{9,8},{10,9... | collective-permute-start | bytes 1572872 | tf_op jit(solution)/shard_map/ppermute | solution.py:296
  159.9 25.4 %copy-start.6 = (s32[1024]{0:T(1024)S(1)}, s32[1024]{0:T(1024)}, u32[]{:S(2)}) copy-start(s32[1024]{0:T(1024)} %param.29) | copy-start | bytes 12292
Sparse Core Ops, SparseCore 0:
  33.5 100.1 all-gather.6
